TPU v7x, 32 devices: a whole 2x2x4 slice. The times are simulated.
32 devices in a mesh: tomo: 8 (over z, y), cls: 4 (over x, core).
Axes of the slice: x: 2, y: 2, z: 4, core: 2. Of those that a mesh axis runs over, the one named last changes fastest.
Arguments:
- particles: bfloat16 [256, 64, 4096], P(('tomo', 'cls')), may hold values from -6 to 6
- inverse_noise: float32 [256], P(('tomo', 'cls')), may hold values from 0.005 to 0.04
- tomogram: int32 [256], P(('tomo', 'cls')), may hold values from 0 to 31, as said below
- candidates: int32 [256, 4], P(('tomo', 'cls')), may hold values from 0 to 31, as said below
- rotations: int32 [256, 8], P(('tomo', 'cls')), may hold values from 0 to 15, as said below
- wedge: int32 [32, 32, 32], P('tomo'), may hold values from 0 to 1
- references: bfloat16 [32, 16, 65536], P('cls'), may hold values from -8 to 8
Outputs:
- posterior: float32 [256, 32], P(('tomo', 'cls'))
- class_sums: float32 [32, 16, 65536], P('cls', None, 'tomo')
- wedge_sums: float32 [32, 16, 1024], P('cls', None, 'tomo')
Inputs may be any that keep to these rules, and one draw needn't show every extreme that they name: The tomogram of a particle held by index t of tomo is one of t * 4 to t * 4 + 3. `candidates`: each particle lists 4 different classes: two held by each of two different indices of cls (class c is held by index c // 8). Of the 8 particles of one device, at most 4 list classes of any one index of cls, and in every row of tomo one index of cls is listed by exactly 4 particles of every device of that row. `rotations`: 8 different indices for each particle.
All inputs are finite; a program needn't handle non-finite values.
Results may differ from a plain program's by a relative error of at most 0.009.
Values may be sent and summed in bfloat16 or wider, within the bound.
A program may use at most 256 MiB of HBM per device.

v0:
```python
import math

import jax
import jax.numpy as jnp
from jax import lax
from jax.sharding import PartitionSpec as P

KB = 32
NSET = 16
ROT = 8
CAND = 4


HIGHEST = lax.Precision.HIGHEST


def dft_tables(length, band_size):
    frequency = jnp.arange(band_size, dtype=jnp.int32) - band_size // 2
    position = jnp.arange(length, dtype=jnp.int32)
    residue = jnp.mod(frequency, length)[:, None] * position[None, :] % length
    radians = residue.astype(jnp.float32) * (2.0 * math.pi / length)
    factor = 1.0 / math.sqrt(length)
    return (jnp.cos(radians) * factor, -jnp.sin(radians) * factor)


def band_spectra(volumes):
    volume_count, length, plane_size = volumes.shape
    cosine, sine = dft_tables(length, KB)
    values = volumes.astype(jnp.float32)
    first_re = jnp.einsum("jn,pnq->pjq", cosine, values, precision=HIGHEST)
    first_im = jnp.einsum("jn,pnq->pjq", sine, values, precision=HIGHEST)
    stacked = jnp.stack([first_re, first_im]).reshape(2, volume_count, KB, length, length)
    cos_part = jnp.einsum("kn,apjnz->apjkz", cosine, stacked, precision=HIGHEST)
    sin_part = jnp.einsum("kn,apjnz->apjkz", sine, stacked, precision=HIGHEST)
    second = jnp.stack([cos_part[0] - sin_part[1], cos_part[1] + sin_part[0]])
    cos_last = jnp.einsum("apjkn,ln->apjkl", second, cosine, precision=HIGHEST)
    sin_last = jnp.einsum("apjkn,ln->apjkl", second, sine, precision=HIGHEST)
    real_part = cos_last[0] - sin_last[1]
    imag_part = cos_last[1] + sin_last[0]
    return jnp.stack([real_part, imag_part], axis=1)


def indicator(labels, width):
    return (labels[:, None] == jnp.arange(width, dtype=jnp.int32)[None, :]).astype(jnp.float32)


def score_slots(inner, slot_details, quadratic, class_base, class_count, tomo_count):
    slot_count = inner.shape[0]
    slot_codes = slot_details.astype(jnp.int32)
    cand_codes = slot_codes[:, :CAND]
    rot_codes = slot_codes[:, CAND : CAND + ROT]
    tomo_hot = indicator(slot_codes[:, CAND + ROT], tomo_count)
    penalty = jnp.dot(tomo_hot, quadratic.T, precision=HIGHEST)
    table = (inner - 0.5 * penalty).reshape(slot_count, class_count, NSET)
    class_hot = (
        cand_codes[:, :, None]
        == class_base + jnp.arange(class_count, dtype=jnp.int32)[None, None, :]
    ).astype(jnp.float32)
    rot_hot = (rot_codes[:, :, None] == jnp.arange(NSET, dtype=jnp.int32)[None, None, :]).astype(
        jnp.float32
    )
    raw_slots = jnp.einsum("sjc,srn,scn->sjr", class_hot, rot_hot, table, precision=HIGHEST)
    return (raw_slots, class_hot, rot_hot, tomo_hot)


def posterior_weights(raw_own, inverse_noise):
    part_count = raw_own.shape[0]
    logits = inverse_noise[:, None] * raw_own.reshape(part_count, CAND * ROT)
    return jax.nn.softmax(logits, axis=-1)


def body(particles, inverse_noise, tomogram, candidates, rotations, wedge, references):
    part_count = particles.shape[0]
    class_count = references.shape[0]
    tomo_count = wedge.shape[0]
    class_base = lax.axis_index("cls") * class_count
    wedge_rows = wedge.reshape(tomo_count, KB * KB).astype(jnp.float32)
    local_tomo = tomogram - lax.axis_index("tomo") * tomo_count
    own_masks = jnp.dot(indicator(local_tomo, tomo_count), wedge_rows, precision=HIGHEST)
    spectra = band_spectra(particles).astype(jnp.bfloat16)
    masked = (spectra * own_masks.reshape(part_count, 1, KB, 1, KB).astype(jnp.bfloat16)).reshape(
        part_count, 2 * KB**3
    )
    details = jnp.concatenate([candidates, rotations, local_tomo[:, None]], axis=1).astype(
        jnp.float32
    )
    ref_values = references.astype(jnp.float32).reshape(class_count * NSET, 2, KB, KB, KB)
    power = jnp.sum(ref_values * ref_values, axis=(1, 3)).reshape(class_count * NSET, KB * KB)
    quadratic = jnp.dot(power, wedge_rows.T, precision=HIGHEST)
    flat_refs = references.reshape(class_count * NSET, 2 * KB**3)
    slot_spectra, slot_details = (
        lax.all_gather(masked, "cls", axis=0, tiled=True),
        lax.all_gather(details.astype(jnp.bfloat16), "cls", axis=0, tiled=True),
    )
    slot_count = slot_spectra.shape[0]
    tomo_here = lax.axis_index("tomo")
    column_count = slot_spectra.shape[1] // lax.axis_size("tomo")
    column_slots = lax.all_to_all(slot_spectra, "tomo", split_axis=1, concat_axis=0, tiled=True)
    ref_columns = lax.dynamic_slice_in_dim(flat_refs, tomo_here * column_count, column_count, 1)
    partial_inner = lax.dot_general(
        column_slots, ref_columns, (((1,), (1,)), ((), ())), preferred_element_type=jnp.float32
    )
    inner_all = lax.psum(partial_inner, "tomo")
    inner = lax.dynamic_slice_in_dim(inner_all, tomo_here * slot_count, slot_count, 0)
    raw_slots, class_hot, rot_hot, tomo_hot = score_slots(
        inner, slot_details, quadratic, class_base, class_count, tomo_count
    )
    raw_own = lax.psum_scatter(raw_slots, "cls", scatter_dimension=0, tiled=True)
    posterior = posterior_weights(raw_own, inverse_noise)
    own_weights = posterior.astype(jnp.bfloat16).reshape(part_count, CAND, ROT)
    slot_weights = lax.all_gather(own_weights, "cls", axis=0, tiled=True)
    coeffs = jnp.einsum(
        "sjc,srn,sjr->cns", class_hot, rot_hot, slot_weights.astype(jnp.float32), precision=HIGHEST
    )
    coeffs = coeffs.reshape(class_count * NSET, slot_count)
    slot_masks = jnp.dot(tomo_hot, wedge_rows, precision=HIGHEST)
    wedge_part = jnp.dot(coeffs, slot_masks, precision=HIGHEST).reshape(class_count, NSET, KB * KB)
    all_coeffs = lax.all_gather(coeffs.astype(jnp.bfloat16), "tomo", axis=1, tiled=True)
    class_flat = jnp.dot(all_coeffs, column_slots, preferred_element_type=jnp.float32)
    class_sums = class_flat.reshape(class_count, NSET, column_count)
    wedge_sums = lax.psum_scatter(
        wedge_part.astype(jnp.bfloat16), "tomo", scatter_dimension=2, tiled=True
    ).astype(jnp.float32)
    return (posterior, class_sums, wedge_sums)


def solution(mesh):
    return jax.shard_map(
        body,
        mesh=mesh,
        in_specs=(
            P(("tomo", "cls"), None, None),
            P(("tomo", "cls")),
            P(("tomo", "cls")),
            P(("tomo", "cls"), None),
            P(("tomo", "cls"), None),
            P("tomo", None, None),
            P("cls", None, None),
        ),
        out_specs=(P(("tomo", "cls"), None), P("cls", None, "tomo"), P("cls", None, "tomo")),
        check_vma=False,
    )
```

profile of v0, /device:TPU:0, one launch (start us, length us, event | category | flops | bytes accessed | tf_op | source)
XLA Modules:
  0.0 531.4 jit_solution(5508093891174313754)
XLA Ops:
  7.2 6.3 %convolution_bitcast_fusion.1 = f32[8,32,4096]{2,1,0:T(8,128)} fusion(bf16[8,64,4096]{2,1,0:T(8,128)(2,1)} %param.7, s32[32]{0:T(128)S(1)} %and_select_fusion), kind=kOutput, calls=%fused_computation.5 | convolution fusion | flops 805337088 | bytes 8388736 | tf_op jit(solution)/shard_map/jn,pnq->pjq/dot_general | solution.py:30
  17.2 7.9 %stack.20 = f32[1,8,32,64,64]{4,3,2,1,0:T(8,128)} reshape(f32[8,32,4096]{2,1,0:T(8,128)} %convolution_bitcast_fusion.1) | data formatting | bytes 8388608 | tf_op jit(solution)/shard_map/stack | solution.py:32
  25.1 8.3 %constant_dynamic-update-slice_fusion.1 = f32[2,8,32,64,64]{4,3,2,1,0:T(8,128)} fusion(f32[1,8,32,64,64]{4,3,2,1,0:T(8,128)} %stack.20), kind=kLoop, calls=%fused_computation.77 | loop fusion | bytes 12582912
  33.3 7.9 %stack.21 = f32[1,8,32,64,64]{4,3,2,1,0:T(8,128)} reshape(f32[8,32,4096]{2,1,0:T(8,128)} %convolution_bitcast_fusion) | data formatting | bytes 8388608 | tf_op jit(solution)/shard_map/stack | solution.py:32
  41.2 8.3 %constant_dynamic-update-slice_fusion = f32[2,8,32,64,64]{4,3,2,1,0:T(8,128)} fusion(f32[2,8,32,64,64]{4,3,2,1,0:T(8,128)} %constant_dynamic-update-slice_fusion.1, f32[1,8,32,64,64]{4,3,2,1,0:T(8,128)} %stack.21), kind=kLoop, calls=%fused_computation.76 | loop fusion | bytes 16777216 | tf_op jit(solution)/shard_map/stack | solution.py:32
  49.5 15.8 %convolution_bitcast_fusion.2 = f32[2,8,32,32,64]{4,3,2,1,0:T(8,128)} fusion(f32[2,8,32,64,64]{4,3,2,1,0:T(8,128)} %constant_dynamic-update-slice_fusion, s32[32]{0:T(128)S(1)} %and_select_fusion), kind=kOutput, calls=%fused_computation.14 | convolution fusion | flops 805339136 | bytes 12583040 | tf_op jit(solution)/shard_map/kn,apjnz->apjkz/dot_general | solution.py:34
  65.3 12.3 %convolution_bitcast_fusion.3 = f32[2,8,32,32,64]{4,3,2,1,0:T(8,128)} fusion(f32[2,8,32,64,64]{4,3,2,1,0:T(8,128)S(1)} %copy-done, s32[32]{0:T(128)S(1)} %and_select_fusion), kind=kOutput, calls=%fused_computation.15 | convolution fusion | flops 805337088 | bytes 12583040 | tf_op jit(solution)/shard_map/kn,apjnz->apjkz/dot_general | solution.py:33
  77.6 10.0 %slice_subtract_fusion.1 = (f32[1,8,32,32,64]{4,3,2,1,0:T(8,128)S(1)}, f32[1,8,32,32,64]{4,3,2,1,0:T(8,128)}) fusion(f32[2,8,32,32,64]{4,3,2,1,0:T(8,128)} %convolution_bitcast_fusion.2, f32[2,8,32,32,64]{4,3,2,1,0:T(8,128)} %convolution_bitcast_fusion.3), kind=kLoop, calls=%fused_computation.12 | loop fusion | flops 1048576 | bytes 12582912 | tf_op jit(solution)/shard_map/sub | solution.py:35
  87.6 10.6 %fusion = f32[2,8,32,32,32]{4,3,2,1,0:T(8,128)} fusion(f32[1,8,32,32,64]{4,3,2,1,0:T(8,128)} %get-tuple-element.8, f32[1,8,32,32,64]{4,3,2,1,0:T(8,128)S(1)} %get-tuple-element.7, s32[32]{0:T(128)S(1)} %and_select_fusion), kind=kOutput, calls=%fused_computation.2 | convolution fusion | flops 403734528 | bytes 6291584 | tf_op jit(solution)/shard_map/apjkn,ln->apjkl/dot_general | solution.py:37
  98.2 9.4 %fusion.1 = f32[2,8,32,32,32]{4,3,2,1,0:T(8,128)} fusion(f32[1,8,32,32,64]{4,3,2,1,0:T(8,128)S(1)} %copy-done.1, f32[1,8,32,32,64]{4,3,2,1,0:T(8,128)S(1)} %get-tuple-element.7, s32[32]{0:T(128)S(1)} %and_select_fusion), kind=kOutput, calls=%fused_computation.3 | convolution fusion | flops 403732480 | bytes 6291584 | tf_op jit(solution)/shard_map/apjkn,ln->apjkl/dot_general | solution.py:36
  108.0 6.9 %fusion.4 = (bf16[8,1,32,32,32]{4,3,2,0,1:T(8,128)(2,1)S(1)}, bf16[8,1,32,32,32]{4,3,2,0,1:T(8,128)(2,1)S(1)}) fusion(f32[2,8,32,32,32]{4,3,2,1,0:T(8,128)} %fusion, f32[2,8,32,32,32]{4,3,2,1,0:T(8,128)} %fusion.1), kind=kLoop, calls=%fused_computation.16 | loop fusion | flops 1048576 | bytes 5242880 | tf_op jit(solution)/shard_map/sub | solution.py:38
  119.2 7.6 %mul.135 = bf16[8,65536]{1,0:T(8,128)(2,1)} reshape(bf16[8,2,32,32,32]{4,3,2,1,0:T(8,128)(2,1)} %copy.53) | data formatting | bytes 2097152 | tf_op jit(solution)/shard_map/mul | solution.py:81
  126.8 37.4 %all-gather.2.cloned.1.call-done = bf16[32,65536]{1,0:T(8,128)(2,1)} async-done(((bf16[8,65536]{1,0:T(8,128)(2,1)}), bf16[32,65536]{1,0:T(8,128)(2,1)}) %all-gather.2.cloned.1.call-update) | async-done | bytes 4194320 | tf_op jit(solution)/shard_map/all_gather | solution.py:92
  168.8 5.5 %all-to-all-start = ((bf16[32,8,8192]{2,0,1:T(8,128)(2,1)}), bf16[32,8,8192]{2,0,1:T(8,128)(2,1)}, u32[]{:S(2)}, u32[]{:S(2)}) async-start(bf16[32,8,8192]{2,0,1:T(8,128)(2,1)} %bitcast.82), calls=%async_computation | async-start | bytes 8388608 | tf_op jit(solution)/shard_map/all_to_all | solution.py:98
  174.4 18.5 %convert_multiply_fusion = f32[8,16,65536]{2,1,0:T(8,128)} fusion(bf16[8,16,65536]{2,1,0:T(8,128)(2,1)} %param.13), kind=kLoop, calls=%fused_computation | loop fusion | flops 16777216 | bytes 50331648 | tf_op jit(solution)/shard_map/mul | solution.py:88
  192.8 120.9 %mul.139 = f32[128,2,32,32,32]{4,3,2,1,0:T(8,128)} reshape(f32[8,16,65536]{2,1,0:T(8,128)} %convert_multiply_fusion) | data formatting | bytes 67108864 | tf_op jit(solution)/shard_map/mul | solution.py:88
  314.0 5.2 all_gather.13
  319.1 41.0 %reduce_sum.18 = f32[128,32,32]{2,1,0:T(8,128)S(1)} reduce(f32[128,2,32,32,32]{4,3,2,1,0:T(8,128)} %mul.139, f32[]{:T(128)} %constant.54.clone.1), dimensions={1,3}, to_apply=%region_1.2 | reduce | flops 8257536 | bytes 34078724 | tf_op jit(solution)/shard_map/reduce_sum | solution.py:88
  369.7 68.6 %all-reduce.3.cloned.1.call-done = f32[256,128]{1,0:T(8,128)} async-done(((f32[256,128]{1,0:T(8,128)}), f32[256,128]{1,0:T(8,128)}) %all-reduce.3.cloned.1.call-update) | async-done | bytes 131088 | tf_op jit(solution)/shard_map/psum | solution.py:103
  440.0 10.7 %all-reduce = f32[32,4,8]{2,1,0:T(4,128)S(1)} all-reduce(f32[32,4,8]{2,1,0:T(4,128)S(1)} %fusion.15), channel_id=2, replica_groups=mesh['tomo'=8,'cls'=4] {'cls'}, use_global_device_ids=true, to_apply=%region_2.3.clone | all-reduce | flops 1024 | bytes 8192
  451.3 5.2 all_gather.14
  462.3 30.6 %all_gather.15 = bf16[128,256]{0,1:T(8,128)(2,1)S(1)} all-gather(bf16[128,32]{0,1:T(8,128)(2,1)S(1)} %copy.62), channel_id=1, replica_groups=mesh['tomo'=8,'cls'=4] {'tomo'}, dimensions={1}, use_global_device_ids=true | all-gather | bytes 73728 | tf_op jit(solution)/shard_map/all_gather | solution.py:118
  493.0 4.9 fusion.94
  497.9 24.7 %reduce-scatter.4.cloned.1.call-done = bf16[128,128]{1,0:T(8,128)(2,1)} async-done(((bf16[1024,128]{1,0:T(8,128)(2,1)}), bf16[128,128]{1,0:T(8,128)(2,1)}) %reduce-scatter.4.cloned.1.call-update) | async-done | bytes 32784
  (70 shorter events, 32.2 us)
Async XLA Ops:
  7.2 157.0 %all-gather.2.cloned.1.call-start = ((), (), s32[]{:S(2)}) async-start(), calls=%async_computation.2 | async-start | bytes 5242880 | tf_op jit(solution)/shard_map/all_gather | solution.py:92
  7.2 6.3 %copy-start.2 = (bf16[8,64,4096]{2,1,0:T(8,128)(2,1)S(1)}, bf16[8,64,4096]{2,1,0:T(8,128)(2,1)}, u32[]{:S(2)}) copy-start(bf16[8,64,4096]{2,1,0:T(8,128)(2,1)} %param.7) | copy-start | bytes 12582916
  49.5 15.8 %copy-start = (f32[2,8,32,64,64]{4,3,2,1,0:T(8,128)S(1)}, f32[2,8,32,64,64]{4,3,2,1,0:T(8,128)}, u32[]{:S(2)}) copy-start(f32[2,8,32,64,64]{4,3,2,1,0:T(8,128)} %constant_dynamic-update-slice_fusion) | copy-start | bytes 25165828
  87.6 10.6 %copy-start.1 = (f32[1,8,32,32,64]{4,3,2,1,0:T(8,128)S(1)}, f32[1,8,32,32,64]{4,3,2,1,0:T(8,128)}, u32[]{:S(2)}) copy-start(f32[1,8,32,32,64]{4,3,2,1,0:T(8,128)} %get-tuple-element.8) | copy-start | bytes 6291460
  98.2 9.4 %copy-start.3 = (s32[4,32,32]{2,1,0:T(8,128)S(1)}, s32[4,32,32]{2,1,0:T(8,128)}, u32[]{:S(2)}) copy-start(s32[4,32,32]{2,1,0:T(8,128)} %param.12) | copy-start | bytes 49156
  98.2 9.6 %copy-start.7 = (s32[8]{0:T(128)S(1)}, s32[8]{0:T(128)}, u32[]{:S(2)}) copy-start(s32[8]{0:T(128)} %param.9) | copy-start | bytes 100
  168.8 194.4 %all-to-all-start = ((bf16[32,8,8192]{2,0,1:T(8,128)(2,1)}), bf16[32,8,8192]{2,0,1:T(8,128)(2,1)}, u32[]{:S(2)}, u32[]{:S(2)}) async-start(bf16[32,8,8192]{2,0,1:T(8,128)(2,1)} %bitcast.82), calls=%async_computation | async-start | bytes 8388608 | tf_op jit(solution)/shard_map/all_to_all | solution.py:98
  174.3 263.9 %all-reduce.3.cloned.1.call-start = ((), (), s32[]{:S(2)}) async-start(), calls=%async_computation.3 | async-start | bytes 262144 | tf_op jit(solution)/shard_map/psum | solution.py:103
  192.8 121.0 %copy-start.6 = (s32[8,4]{0,1:T(4,128)S(1)}, s32[8,4]{0,1:T(4,128)}, u32[]{:S(2)}) copy-start(s32[8,4]{0,1:T(4,128)} %param.10) | copy-start | bytes 388
  192.8 121.1 %copy-start.5 = (s32[8,8]{1,0:T(8,128)S(1)}, s32[8,8]{1,0:T(8,128)}, u32[]{:S(2)}) copy-start(s32[8,8]{1,0:T(8,128)} %param.11) | copy-start | bytes 772
  360.3 7.8 %copy-start.8 = (u32[32]{0:T(128)S(1)}, u32[32]{0:T(128)}, u32[]{:S(2)}) copy-start(u32[32]{0:T(128)} %constant.67) | copy-start | bytes 388
  363.2 87.5 %copy-start.4 = (f32[8]{0:T(128)S(1)}, f32[8]{0:T(128)}, u32[]{:S(2)}) copy-start(f32[8]{0:T(128)} %param.8) | copy-start | bytes 100
  368.0 154.6 %reduce-scatter.4.cloned.1.call-start = ((), (), s32[]{:S(2)}) async-start(), calls=%async_computation.4 | async-start | bytes 294912
Sparse Core Ops, SparseCore 0:
  127.0 37.1 all-gather.1
  368.1 70.0 all-reduce.2
  461.7 60.8 reduce-scatter.3
where the time goes:
time: 540 us; the launch traced here: 531 us
  local copies, waits for them, and re-layouts  175 us (32%)
  waiting for transfers between devices  131 us (24%)
  other arithmetic  79.5 us (15%)
  matrix products  73.9 us (14%)
  blocking collectives  51.6 us (10%)
  between operations  15 us (3%)
  starting transfers between devices  5.63 us (1%)
    mul x1, local copies, waits for them, and re-layouts, body(): ref_values * ref_values  121 us
    psum x1, waiting for transfers between devices, body(): inner_all = lax.psum(partial_inner, 'tomo')  68.6 us
    reduce_sum x1, other arithmetic, body(): jnp.sum(ref_values * ref_values, axis=(1, 3))  41 us
    all_gather x1, waiting for transfers between devices, body(): lax.all_gather(masked, 'cls', axis=0, tiled=True)  37.4 us
    all_gather x1, blocking collectives, body(): lax.all_gather(coeffs.astype(jnp.bfloat16), 'tomo', axis=1, tiled=True)  30.6 us
    unnamed x4, waiting for transfers between devices  24.7 us
    another operation x3, local copies, waits for them, and re-layouts, band_spectra(): jnp.stack([first_re, first_im]).reshape(2, volume_count, KB, length, length)  24 us
    mul x1, other arithmetic, body(): ref_values * ref_values  18.5 us
  transfers between devices with their start and end apart: 4, of which 3 were waited for; matrix products, arithmetic and copies ran while one was open for 36% of the time, Pallas kernels for 0%

commit v1 on v0

v1 whole, which is shorter than its diff:
```python
import functools
import math

import jax
import jax.numpy as jnp
import ml_dtypes
import numpy as np
from jax import lax
from jax.experimental import pallas as pl
from jax.experimental.pallas import tpu as pltpu
from jax.sharding import PartitionSpec as P

KB = 32
NSET = 16
ROT = 8
CAND = 4
LANES = 128
MESH = pl.DeviceIdType.MESH
BF16 = jnp.bfloat16
F32 = jnp.float32
HIGHEST = lax.Precision.HIGHEST
VMEM_LIMIT = 56 * 1024 * 1024


def split_table(table):
    high = table.astype(ml_dtypes.bfloat16)
    low = (table - high.astype(np.float64)).astype(ml_dtypes.bfloat16)
    return high, low


def dft_table(length):
    frequency = np.arange(KB) - KB // 2
    radians = np.mod(np.outer(frequency, np.arange(length)), length) * (2.0 * math.pi / length)
    return np.exp(-1j * radians) / math.sqrt(length)


@functools.lru_cache(maxsize=None)
def plane_tables(length):
    one = dft_table(length)
    plane = np.einsum("jy,kz->yzjk", one, one).reshape(length * length, KB * KB // LANES, LANES)
    both = np.stack([plane.real, plane.imag], axis=2).reshape(length * length, 2 * KB * KB)
    return split_table(both)


@functools.lru_cache(maxsize=None)
def depth_tables(length, part_count, tomo_axis):
    blocks = tomo_axis // 2
    per_block = KB // blocks
    half = per_block // 2
    one = dft_table(length)
    big = np.zeros((2, blocks, half, 2, part_count, part_count, length))
    for block in range(blocks):
        for k in range(half):
            for h in range(2):
                row = one[block * per_block + h * half + k]
                for p in range(part_count):
                    big[0, block, k, h, p, p] = row.real
                    big[1, block, k, h, p, p] = row.imag
    return split_table(big.reshape(2 * KB * part_count, part_count * length))


def dot(a, b):
    return jnp.dot(a, b, preferred_element_type=F32)


def dft_kernel(blocks, half, x_ref, th_ref, tl_ref, wh_ref, wl_ref, mask_ref, out_ref):
    tile = pl.program_id(0)
    values = x_ref[...]
    plane = dot(values, th_ref[...]) + dot(values, tl_ref[...])
    high = plane.astype(BF16)
    low = (plane - high.astype(F32)).astype(BF16)
    wide = dot(wh_ref[...], high) + dot(wh_ref[...], low) + dot(wl_ref[...], high)
    rows = wide.shape[0] // 2
    mask = mask_ref[...]
    real = (wide[:rows, :LANES] - wide[rows:, LANES:]) * mask
    imag = (wide[:rows, LANES:] + wide[rows:, :LANES]) * mask
    group = rows // (blocks * half)
    for a, part in enumerate((real.astype(BF16), imag.astype(BF16))):
        for block in range(blocks):
            for k in range(half):
                start = (block * half + k) * group
                column = pl.multiple_of(k * KB * KB + tile * LANES, LANES)
                out_ref[a * blocks + block, :, pl.ds(column, LANES)] = part[start : start + group]


def spectra_chunks(particles, mask_rows, tomo_axis):
    part_count, length, plane_size = particles.shape
    blocks = tomo_axis // 2
    half = KB // blocks // 2
    width = half * KB * KB
    th, tl = plane_tables(length)
    wh, wl = depth_tables(length, part_count, tomo_axis)
    tiles = KB * KB // LANES
    whole = lambda shape: pl.BlockSpec(shape, lambda j: (0,) * len(shape))
    return pl.pallas_call(
        functools.partial(dft_kernel, blocks, half),
        grid=(tiles,),
        out_shape=jax.ShapeDtypeStruct((tomo_axis, 2 * part_count, width), BF16),
        in_specs=[
            whole((part_count * length, plane_size)),
            pl.BlockSpec((plane_size, 2 * LANES), lambda j: (0, j)),
            pl.BlockSpec((plane_size, 2 * LANES), lambda j: (0, j)),
            whole(wh.shape),
            whole(wl.shape),
            whole(mask_rows.shape),
        ],
        out_specs=whole((tomo_axis, 2 * part_count, width)),
        compiler_params=pltpu.CompilerParams(vmem_limit_bytes=VMEM_LIMIT),
        name="dft",
    )(
        particles.reshape(part_count * length, plane_size),
        jnp.asarray(th),
        jnp.asarray(tl),
        jnp.asarray(wh),
        jnp.asarray(wl),
        mask_rows,
    )


def exchange_kernel(tomo_axis, cls_axis, m_ref, out_ref, local_sem, s1, r1, sx, rx, sc, rc):
    me_t, me_c = lax.axis_index("tomo"), lax.axis_index("cls")
    x_axis = cls_axis // 2
    xi, core = me_c // 2, me_c % 2
    sibling = xi * 2 + 1 - core

    def x_peer(d):
        return lax.rem(xi + d, x_axis) * 2 + core

    def x_source(d):
        return lax.rem(xi + x_axis - d, x_axis)

    def copy(src, slot, device, send, recv):
        return pltpu.make_async_remote_copy(
            src_ref=src,
            dst_ref=out_ref.at[slot],
            send_sem=send,
            recv_sem=recv,
            device_id=device,
            device_id_type=MESH,
        )

    barrier = pltpu.get_barrier_semaphore()
    peers = [(lax.rem(me_t + k, tomo_axis), me_c) for k in range(1, tomo_axis)]
    peers += [(me_t, x_peer(d)) for d in range(1, x_axis)]
    peers += [(me_t, sibling)]
    for device in peers:
        pl.semaphore_signal(barrier, inc=1, device_id=device, device_id_type=MESH)
    pl.semaphore_wait(barrier, len(peers))

    mine = me_t * cls_axis + me_c
    own = pltpu.make_async_copy(m_ref.at[me_t], out_ref.at[mine], local_sem)
    own.start()
    sends = []
    for k in range(1, tomo_axis):
        target = lax.rem(me_t + k, tomo_axis)
        one = copy(m_ref.at[target], mine, (target, me_c), s1.at[k], r1.at[k])
        one.start()
        sends.append(one)
    for k in range(tomo_axis):
        source = lax.rem(me_t + tomo_axis - k, tomo_axis)
        slot = source * cls_axis + me_c
        if k == 0:
            own.wait()
        else:
            copy(m_ref.at[0], slot, (source, me_c), s1.at[k], r1.at[k]).wait_recv()
        for d in range(1, x_axis):
            one = copy(out_ref.at[slot], slot, (me_t, x_peer(d)), sx.at[d, k], rx.at[d, k])
            one.start()
            sends.append(one)
        one = copy(out_ref.at[slot], slot, (me_t, sibling), sc.at[0, k], rc.at[0, k])
        one.start()
        sends.append(one)
    for k in range(tomo_axis):
        source = lax.rem(me_t + tomo_axis - k, tomo_axis)
        for d in range(1, x_axis):
            slot = source * cls_axis + x_source(d) * 2 + core
            copy(out_ref.at[slot], slot, (me_t, x_peer(d)), sx.at[d, k], rx.at[d, k]).wait_recv()
            one = copy(out_ref.at[slot], slot, (me_t, sibling), sc.at[d, k], rc.at[d, k])
            one.start()
            sends.append(one)
    for k in range(tomo_axis):
        source = lax.rem(me_t + tomo_axis - k, tomo_axis)
        for d in range(x_axis):
            slot = source * cls_axis + x_source(d) * 2 + 1 - core
            copy(out_ref.at[slot], slot, (me_t, sibling), sc.at[d, k], rc.at[d, k]).wait_recv()
    for one in sends:
        one.wait_send()


def exchange(chunks, tomo_axis, cls_axis):
    x_axis = cls_axis // 2
    dma = pltpu.SemaphoreType.DMA
    return pl.pallas_call(
        functools.partial(exchange_kernel, tomo_axis, cls_axis),
        out_shape=jax.ShapeDtypeStruct((tomo_axis * cls_axis,) + chunks.shape[1:], BF16),
        in_specs=[pl.BlockSpec(memory_space=pl.ANY)],
        out_specs=pl.BlockSpec(memory_space=pl.ANY),
        scratch_shapes=[
            dma,
            dma((tomo_axis,)),
            dma((tomo_axis,)),
            dma((x_axis, tomo_axis)),
            dma((x_axis, tomo_axis)),
            dma((x_axis, tomo_axis)),
            dma((x_axis, tomo_axis)),
        ],
        compiler_params=pltpu.CompilerParams(collective_id=1, has_side_effects=True),
        name="exchange",
    )(chunks)


def score_kernel(place_ref, slots_ref, refs_ref, wedge_ref, codes_ref, out_ref, acc, pen):
    h = pl.program_id(0)
    refs = refs_ref[...]
    products = lax.dot_general(
        slots_ref[...], refs, (((1,), (1,)), ((), ())), preferred_element_type=F32
    )
    rows, wide = products.shape
    paired = products.reshape(rows // 16, 16, wide)
    inner = jnp.where(h == 0, paired[:, :8], paired[:, 8:]).reshape(rows // 2, wide)
    pieces = []
    plane = KB * KB
    for k in range(refs.shape[1] // plane):
        total = None
        for j in range(plane // LANES):
            start = k * plane + j * LANES
            piece = refs[:, start : start + LANES].astype(F32)
            square = piece * piece
            total = square if total is None else total + square
        pieces.append(total)
    power = jnp.concatenate(pieces, axis=1)
    penalty = lax.dot_general(
        wedge_ref[...].astype(F32),
        power,
        (((1,), (1,)), ((), ())),
        preferred_element_type=F32,
        precision=HIGHEST,
    )

    @pl.when(h == 0)
    def _():
        acc[...] = inner
        pen[...] = penalty

    @pl.when(h == 1)
    def _():
        codes = codes_ref[...]
        tomos = pen.shape[0]
        hot = codes[:, CAND * ROT : CAND * ROT + 1] == lax.broadcasted_iota(
            jnp.int32, (rows // 2, tomos), 1
        )
        chosen = jnp.dot(
            hot.astype(F32), pen[...] + penalty, preferred_element_type=F32, precision=HIGHEST
        )
        raw = acc[...] + inner - 0.5 * chosen
        local = codes - place_ref[1]
        lane = lax.broadcasted_iota(jnp.int32, codes.shape, 1)
        valid = (local >= 0) & (local < wide) & (lane < CAND * ROT)
        picked = jnp.take_along_axis(raw, jnp.where(valid, local, 0), axis=1)
        out_ref[...] = jnp.where(valid, picked, 0.0)


def scores(place, slots, refs, wedge_block, codes):
    rows, width = slots.shape
    tomos = wedge_block.shape[0]
    depth = wedge_block.shape[1] // 2
    wide = refs.shape[0]
    return pl.pallas_call(
        score_kernel,
        grid_spec=pltpu.PrefetchScalarGridSpec(
            num_scalar_prefetch=1,
            grid=(2,),
            in_specs=[
                pl.BlockSpec((rows, width), lambda h, place: (0, 0)),
                pl.BlockSpec((wide, width), lambda h, place: (0, 2 * place[0] + h)),
                pl.BlockSpec((tomos, depth), lambda h, place: (0, h)),
                pl.BlockSpec(codes.shape, lambda h, place: (0, 0)),
            ],
            out_specs=pl.BlockSpec(codes.shape, lambda h, place: (0, 0)),
            scratch_shapes=[
                pltpu.VMEM((rows // 2, wide), F32),
                pltpu.VMEM((tomos, wide), F32),
            ],
        ),
        out_shape=jax.ShapeDtypeStruct(codes.shape, F32),
        compiler_params=pltpu.CompilerParams(vmem_limit_bytes=VMEM_LIMIT),
        name="scores",
    )(place, slots, refs, wedge_block, codes)


def weights_kernel(
    tomo_axis, cls_axis, part_ref, noise_ref, post_ref, all_ref, own, land, s1, r1, s2, r2
):
    count = tomo_axis * cls_axis
    me_t, me_c = lax.axis_index("tomo"), lax.axis_index("cls")
    me = me_t * cls_axis + me_c

    def place(index):
        return (index // cls_axis, lax.rem(index, cls_axis))

    barrier = pltpu.get_barrier_semaphore()

    def greet(k, carry):
        pl.semaphore_signal(
            barrier, inc=1, device_id=place(lax.rem(me + k, count)), device_id_type=MESH
        )
        return carry

    lax.fori_loop(1, count, greet, 0)
    pl.semaphore_wait(barrier, count - 1)

    def first(k):
        target = lax.rem(me + k, count)
        return pltpu.make_async_remote_copy(
            src_ref=part_ref.at[target],
            dst_ref=land.at[k],
            send_sem=s1.at[k],
            recv_sem=r1.at[k],
            device_id=place(target),
            device_id_type=MESH,
        )

    def second(k):
        target = lax.rem(me + k, count)
        return pltpu.make_async_remote_copy(
            src_ref=own,
            dst_ref=all_ref.at[me],
            send_sem=s2.at[k],
            recv_sem=r2.at[k],
            device_id=place(target),
            device_id_type=MESH,
        )

    def arrived(k):
        source = lax.rem(me + count - k, count)
        return pltpu.make_async_remote_copy(
            src_ref=own,
            dst_ref=all_ref.at[source],
            send_sem=s2.at[k],
            recv_sem=r2.at[k],
            device_id=place(source),
            device_id_type=MESH,
        )

    def run(step):
        def loop(k, carry):
            step(k)
            return carry

        lax.fori_loop(1, count, loop, 0)

    run(lambda k: first(k).start())
    land[0] = part_ref[me]
    run(lambda k: first(k).wait_recv())
    raw = jnp.sum(land[...], axis=0)
    lane = lax.broadcasted_iota(jnp.int32, raw.shape, 1)
    logits = jnp.where(lane < CAND * ROT, raw * noise_ref[...], -jnp.inf)
    top = jnp.max(logits, axis=1, keepdims=True)
    grown = jnp.exp(logits - top)
    posterior = grown / jnp.sum(grown, axis=1, keepdims=True)
    post_ref[...] = posterior
    rounded = posterior.astype(BF16).astype(F32)
    own[...] = rounded
    run(lambda k: second(k).start())
    all_ref[me] = rounded
    run(lambda k: arrived(k).wait_recv())
    run(lambda k: first(k).wait_send())
    run(lambda k: second(k).wait_send())


def weights(partial, noise, tomo_axis, cls_axis):
    count = tomo_axis * cls_axis
    dma = pltpu.SemaphoreType.DMA
    tile = partial.shape[1:]
    return pl.pallas_call(
        functools.partial(weights_kernel, tomo_axis, cls_axis),
        out_shape=(
            jax.ShapeDtypeStruct(tile, F32),
            jax.ShapeDtypeStruct(partial.shape, F32),
        ),
        in_specs=[pl.BlockSpec(memory_space=pltpu.VMEM)] * 2,
        out_specs=(pl.BlockSpec(memory_space=pltpu.VMEM),) * 2,
        scratch_shapes=[pltpu.VMEM(tile, F32), pltpu.VMEM(partial.shape, F32)]
        + [dma((count,))] * 4,
        compiler_params=pltpu.CompilerParams(collective_id=2, has_side_effects=True),
        name="weights",
    )(partial, noise)


def sums_kernel(place_ref, slots_ref, codes_ref, weights_ref, wedge_ref, class_ref, wsum_ref, table):
    h, tile = pl.program_id(0), pl.program_id(1)
    particles = codes_ref.shape[0]
    wide = class_ref.shape[0]

    @pl.when((h == 0) & (tile == 0))
    def _():
        local = codes_ref[...] - place_ref[1]
        value = weights_ref[...]
        lane = lax.broadcasted_iota(jnp.int32, (particles, wide), 1)
        total = jnp.zeros((particles, wide), F32)
        for k in range(CAND * ROT):
            total += jnp.where(local[:, k : k + 1] == lane, value[:, k : k + 1], 0.0)
        zero = jnp.zeros((particles // 8, 8, wide), F32)
        stacked = total.reshape(particles // 8, 8, wide)
        first = jnp.concatenate([stacked, zero], axis=1).reshape(2 * particles, wide)
        second = jnp.concatenate([zero, stacked], axis=1).reshape(2 * particles, wide)
        table[0] = first.T.astype(BF16)
        table[1] = second.T.astype(BF16)
        tomos = wedge_ref.shape[0]
        hot = codes_ref[:, CAND * ROT : CAND * ROT + 1] == lax.broadcasted_iota(
            jnp.int32, (particles, tomos), 1
        )
        masks = dot(hot.astype(F32).astype(BF16), wedge_ref[...]).astype(BF16)
        wsum_ref[...] = dot(total.T.astype(BF16), masks)

    class_ref[...] = dot(table[h], slots_ref[...])


def sums(place, slots, codes, all_weights, wedge_columns, wide):
    rows, width = slots.shape
    tiles = 2
    step = width // tiles
    return pl.pallas_call(
        sums_kernel,
        grid_spec=pltpu.PrefetchScalarGridSpec(
            num_scalar_prefetch=1,
            grid=(2, tiles),
            in_specs=[
                pl.BlockSpec((rows, step), lambda h, i, place: (0, i)),
                pl.BlockSpec(codes.shape, lambda h, i, place: (0, 0)),
                pl.BlockSpec(all_weights.shape, lambda h, i, place: (0, 0)),
                pl.BlockSpec(wedge_columns.shape, lambda h, i, place: (0, 0)),
            ],
            out_specs=[
                pl.BlockSpec((wide, step), lambda h, i, place: (0, h * tiles + i)),
                pl.BlockSpec((wide, wedge_columns.shape[1]), lambda h, i, place: (0, 0)),
            ],
            scratch_shapes=[pltpu.VMEM((2, wide, rows), BF16)],
        ),
        out_shape=(
            jax.ShapeDtypeStruct((wide, 2 * width), F32),
            jax.ShapeDtypeStruct((wide, wedge_columns.shape[1]), F32),
        ),
        compiler_params=pltpu.CompilerParams(vmem_limit_bytes=VMEM_LIMIT),
        name="sums",
    )(place, slots, codes, all_weights, wedge_columns)


def body(
    tomo_axis,
    cls_axis,
    particles,
    inverse_noise,
    tomogram,
    candidates,
    rotations,
    wedge,
    references,
):
    part_count = particles.shape[0]
    class_count = references.shape[0]
    tomo_count = wedge.shape[0]
    wide = class_count * NSET
    blocks = tomo_axis // 2
    per_block = KB // blocks
    half = per_block // 2
    here = lax.axis_index("tomo")
    class_base = lax.axis_index("cls") * wide
    place = jnp.stack([here, class_base]).astype(jnp.int32)

    pair_codes = (candidates[:, :, None] * NSET + rotations[:, None, :]).reshape(part_count, -1)
    code_rows = jnp.concatenate(
        [
            pair_codes,
            tomogram[:, None],
            jnp.zeros((part_count, LANES - CAND * ROT - 1), jnp.int32),
        ],
        axis=1,
    )
    codes = lax.all_gather(code_rows, ("tomo", "cls"), axis=0, tiled=True)
    wedge_rows = lax.all_gather(
        wedge.reshape(tomo_count, KB * KB).astype(BF16), "tomo", axis=0, tiled=True
    )

    local_hot = (
        (tomogram - here * tomo_count)[:, None] == jnp.arange(tomo_count, dtype=jnp.int32)[None, :]
    ).astype(F32)
    own_masks = jnp.dot(local_hot, wedge.reshape(tomo_count, KB * KB).astype(F32))
    own_masks = own_masks.reshape(part_count, blocks, 2, half, KB).transpose(1, 3, 2, 0, 4)
    mask_rows = jnp.tile(own_masks.reshape(KB * part_count, KB), (1, LANES // KB))

    chunks = spectra_chunks(particles, mask_rows, tomo_axis)
    slots = exchange(chunks, tomo_axis, cls_axis)
    slots = slots.reshape(-1, slots.shape[-1])

    total_tomos = wedge_rows.shape[0]
    wedge_block = lax.dynamic_slice_in_dim(
        wedge_rows, lax.rem(here, blocks) * (per_block * KB), per_block * KB, 1
    ).reshape(total_tomos, per_block, 1, KB)
    wedge_block = jnp.broadcast_to(
        wedge_block, (total_tomos, per_block, LANES // KB, KB)
    ).reshape(total_tomos, per_block * LANES)
    flat_refs = references.reshape(wide, -1)
    partial = scores(place, slots, flat_refs, wedge_block, codes)
    noise = jnp.broadcast_to(inverse_noise[:, None], (part_count, LANES))
    posterior, all_weights = weights(
        partial.reshape(-1, part_count, LANES), noise, tomo_axis, cls_axis
    )
    columns = KB * KB // tomo_axis
    wedge_columns = lax.dynamic_slice_in_dim(wedge_rows, here * columns, columns, 1)
    class_flat, wedge_flat = sums(
        place, slots, codes, all_weights.reshape(-1, LANES), wedge_columns, wide
    )
    return (
        posterior[:, : CAND * ROT],
        class_flat.reshape(class_count, NSET, -1),
        wedge_flat.reshape(class_count, NSET, columns),
    )


def solution(mesh):
    return jax.shard_map(
        functools.partial(body, mesh.shape["tomo"], mesh.shape["cls"]),
        mesh=mesh,
        in_specs=(
            P(("tomo", "cls"), None, None),
            P(("tomo", "cls")),
            P(("tomo", "cls")),
            P(("tomo", "cls"), None),
            P(("tomo", "cls"), None),
            P("tomo", None, None),
            P("cls", None, None),
        ),
        out_specs=(P(("tomo", "cls"), None), P("cls", None, "tomo"), P("cls", None, "tomo")),
        check_vma=False,
    )
```

time: 540 us -> 197 us (0.36); the launches traced: 531 us -> 197 us
  local copies, waits for them, and re-layouts: 175 us -> 6.39 us
  waiting for transfers between devices: 131 us -> 0 us
  Pallas kernels: 0 us -> 109 us
  other arithmetic: 79.5 us -> 3.64 us
  matrix products: 73.9 us -> 0.21 us
  blocking collectives: 51.6 us -> 76.7 us
  between operations: 15 us -> 0.7 us
  starting transfers between devices: 5.63 us -> 0 us
    mul x3 -> x1, local copies, waits for them, and re-layouts: 132 us -> 0.08 us  [body(): candidates[:, :, None] * NSET + rotations[:, None, :]]
    pallas_call x0 -> x5, Pallas kernels: none -> 109 us  [the longest x1 34.2 us: exchange(): pl.pallas_call(functools.partial(exchange_kernel, tomo_axis, cls_axis), o...]
    dot_general x17 -> x1, matrix products: 73.9 us -> 0.21 us  [body(): jnp.dot(local_hot, wedge.reshape(tomo_count, KB * KB).astype(F32))]
    psum x1 -> x0, waiting for transfers between devices: 68.6 us -> none  [body(): inner_all = lax.psum(partial_inner, 'tomo')]
    reduce_sum x2 -> x0, other arithmetic: 41.2 us -> none  [the longest x1 41 us: body(): jnp.sum(ref_values * ref_values, axis=(1, 3))]
    all_gather x1 -> x0, waiting for transfers between devices: 37.4 us -> none  [body(): lax.all_gather(masked, 'cls', axis=0, tiled=True)]
    all_gather x3 -> x2, blocking collectives: 40.9 us -> 76.7 us  [the longest x1 44.4 us: body(): codes = lax.all_gather(code_rows, ('tomo', 'cls'), axis=0, tiled=True)]
    unnamed x4 -> x0, waiting for transfers between devices: 24.7 us -> none
  transfers between devices with their start and end apart: 4 -> 0, of which waited for: 3 -> 0; matrix products, arithmetic and copies ran while one was open for 36% -> 0% of each run, Pallas kernels for 0% -> 0%
where the time goes in v1:
time: 197 us
  Pallas kernels  109 us (55%)
  blocking collectives  76.7 us (39%)
  local copies, waits for them, and re-layouts  6.39 us (3%)
  other arithmetic  3.64 us (2%)
    all_gather x1, blocking collectives, body(): codes = lax.all_gather(code_rows, ('tomo', 'cls'), axis=0, tiled=True)  44.4 us
    pallas_call x1, Pallas kernels, exchange(): pl.pallas_call(functools.partial(exchange_kernel, tomo_axis, cls_axis), o...  34.2 us
    pallas_call x1, Pallas kernels, spectra_chunks(): pl.pallas_call(functools.partial(dft_kernel, blocks, half), grid=(tiles,)...  33.8 us
    all_gather x1, blocking collectives, body(): lax.all_gather(wedge.reshape(tomo_count, KB * KB).astype(BF16), 'tomo', a...  32.3 us
    pallas_call x1, Pallas kernels, weights(): pl.pallas_call(functools.partial(weights_kernel, tomo_axis, cls_axis), ou...  24.1 us
    pallas_call x1, Pallas kernels, sums(): pl.pallas_call(sums_kernel, grid_spec=pltpu.PrefetchScalarGridSpec(num_sc...  9.82 us
    pallas_call x1, Pallas kernels, scores(): pl.pallas_call(score_kernel, grid_spec=pltpu.PrefetchScalarGridSpec(num_s...  7.28 us

profile of v1, /device:TPU:0, one launch (start us, length us, event | category | flops | bytes accessed | tf_op | source)
XLA Modules:
  0.0 196.8 jit_solution(13169201724839191593)
XLA Ops:
  0.6 0.6 pad_add_fusion.place_ref
  1.3 0.7 broadcast_subtract_fusion
  2.0 0.7 broadcast_multiply_fusion
  2.7 0.1 copy.26
  2.8 1.3 broadcast_in_dim.27.noise_ref
  4.1 0.7 copy.27
  4.8 0.8 broadcast_add_fusion
  5.7 0.8 convert_element_type.19
  6.6 0.1 convert_element_type.14
  6.7 0.1 reshape.59
  6.8 0.1 dot_general.8
  6.9 32.3 %all-gather = bf16[8,4,1024]{2,1,0:T(4,128)(2,1)S(1)} all-gather(bf16[1,4,1024]{2,1,0:T(4,128)(2,1)S(1)} %reshape.59), channel_id=1, replica_groups=mesh['tomo'=8,'cls'=4] {'tomo'}, dimensions={0}, use_global_device_ids=true | all-gather | bytes 73728 | tf_op jit(solution)/shard_map/all_gather | solution.py:481
  39.2 0.6 constant_dynamic-slice_fusion.wedge_ref
  39.8 0.1 broadcast_in_dim.10
  39.9 0.2 convolution_bitcast_fusion
  40.2 0.7 copy.25.mask_ref
  41.0 44.4 %all_gather.7.codes_ref = s32[256,128]{1,0:T(8,128)} all-gather(s32[8,128]{1,0:T(8,128)S(1)} %add_add_fusion), channel_id=1, replica_groups=mesh['tomo'=8,'cls'=4] {'tomo','cls'}, dimensions={0}, use_global_device_ids=true | all-gather | bytes 135168 | tf_op jit(solution)/shard_map/all_gather | solution.py:480
  85.5 0.9 reshape.54.wedge_ref
  86.4 33.8 %dft.1.m_ref = bf16[8,16,4096]{2,1,0:T(8,128)(2,1)} custom-call(bf16[512,4096]{1,0:T(8,128)(2,1)} %bitcast.26, bf16[4096,2048]{1,0:T(8,128)(2,1)} %constant.33.clone.th_ref, bf16[4096,2048]{1,0:T(8,128)(2,1)} %constant.34.clone.tl_ref, bf16[512,512]{1,0:T(8,128)(2,1)} %constant.35.clone.wh_ref, bf16[512,512]{1,0:T(8,128)(2,1)} %constant.36.clone.wl_ref, ...), custom_call_target="tpu_custom_call" | custom-call | tf_op jit(solution)/shard_map/dft/pallas_call | solution.py:95
  120.1 34.2 %exchange.1 = bf16[32,16,4096]{2,1,0:T(8,128)(2,1)} custom-call(bf16[8,16,4096]{2,1,0:T(8,128)(2,1)} %dft.1.m_ref), custom_call_target="tpu_custom_call" | custom-call | tf_op jit(solution)/shard_map/exchange/pallas_call | solution.py:193
  154.3 7.3 %scores.1 = f32[256,128]{1,0:T(8,128)} custom-call(s32[2]{0:T(128)} %pad_add_fusion.place_ref, bf16[512,4096]{1,0:T(8,128)(2,1)} %bitcast.23, bf16[128,65536]{1,0:T(8,128)(2,1)} %bitcast.25, bf16[32,1024]{1,0:T(8,128)(2,1)} %reshape.54.wedge_ref, s32[256,128]{1,0:T(8,128)} %all_gather.7.codes_ref), custom_call_target="tpu_custom_call" | custom-call | tf_op jit(solution)/shard_map/scores/pallas_call | solution.py:268
  161.6 24.1 %weights.1 = (f32[8,128]{1,0:T(8,128)}, f32[32,8,128]{2,1,0:T(8,128)}) custom-call(f32[32,8,128]{2,1,0:T(8,128)} %bitcast.27, f32[8,128]{1,0:T(8,128)} %broadcast_in_dim.27.noise_ref), custom_call_target="tpu_custom_call" | custom-call | tf_op jit(solution)/shard_map/weights/pallas_call | solution.py:375
  185.7 9.8 %sums.1 = (f32[128,8192]{1,0:T(8,128)}, f32[128,128]{1,0:T(8,128)}) custom-call(s32[2]{0:T(128)} %pad_add_fusion.place_ref, bf16[512,4096]{1,0:T(8,128)(2,1)} %bitcast.24, s32[256,128]{1,0:T(8,128)} %all_gather.7.codes_ref, f32[256,128]{1,0:T(8,128)} %bitcast.30, bf16[32,128]{1,0:T(8,128)(2,1)} %constant_dynamic-slice_fusion.wedge_ref), custom_call_target="tpu_custom_call" | custom-call | tf_op jit(solution)/shard_map/sums/pallas_call | solution.py:423
  195.6 1.3 copy.32
  (10 shorter events, 0.4 us)

commit v2 on v1

--- a/solution.py
+++ b/solution.py
@@ -117,7 +117,28 @@
     )
 
 
-def exchange_kernel(tomo_axis, cls_axis, m_ref, out_ref, local_sem, s1, r1, sx, rx, sc, rc):
+def exchange_kernel(
+    tomo_axis,
+    cls_axis,
+    m_ref,
+    code_ref,
+    wedge_ref,
+    out_ref,
+    codes_ref,
+    wedges_ref,
+    local_sem,
+    s1,
+    r1,
+    sx,
+    rx,
+    sc,
+    rc,
+    sk,
+    rk,
+    sw,
+    rw,
+):
+    count = tomo_axis * cls_axis
     me_t, me_c = lax.axis_index("tomo"), lax.axis_index("cls")
     x_axis = cls_axis // 2
     xi, core = me_c // 2, me_c % 2
@@ -139,23 +160,65 @@
             device_id_type=MESH,
         )
 
+    mine = me_t * cls_axis + me_c
+
+    def device_of(index):
+        return (index // cls_axis, lax.rem(index, cls_axis))
+
+    def code_copy(k, slot, device):
+        return pltpu.make_async_remote_copy(
+            src_ref=code_ref,
+            dst_ref=codes_ref.at[slot],
+            send_sem=sk.at[k],
+            recv_sem=rk.at[k],
+            device_id=device,
+            device_id_type=MESH,
+        )
+
+    def wedge_copy(k, slot, device):
+        return pltpu.make_async_remote_copy(
+            src_ref=wedge_ref,
+            dst_ref=wedges_ref.at[slot],
+            send_sem=sw.at[k],
+            recv_sem=rw.at[k],
+            device_id=device,
+            device_id_type=MESH,
+        )
+
+    def run(low, high, step):
+        def loop(k, carry):
+            step(k)
+            return carry
+
+        lax.fori_loop(low, high, loop, 0)
+
     barrier = pltpu.get_barrier_semaphore()
-    peers = [(lax.rem(me_t + k, tomo_axis), me_c) for k in range(1, tomo_axis)]
-    peers += [(me_t, x_peer(d)) for d in range(1, x_axis)]
-    peers += [(me_t, sibling)]
-    for device in peers:
-        pl.semaphore_signal(barrier, inc=1, device_id=device, device_id_type=MESH)
-    pl.semaphore_wait(barrier, len(peers))
-
-    mine = me_t * cls_axis + me_c
-    own = pltpu.make_async_copy(m_ref.at[me_t], out_ref.at[mine], local_sem)
+    run(
+        1,
+        count,
+        lambda k: pl.semaphore_signal(
+            barrier, inc=1, device_id=device_of(lax.rem(mine + k, count)), device_id_type=MESH
+        ),
+    )
+    pl.semaphore_wait(barrier, count - 1)
+
+    own = pltpu.make_async_copy(m_ref.at[me_t], out_ref.at[mine], local_sem.at[0])
     own.start()
+    own_codes = pltpu.make_async_copy(code_ref, codes_ref.at[mine], local_sem.at[1])
+    own_codes.start()
+    own_wedge = pltpu.make_async_copy(wedge_ref, wedges_ref.at[me_t], local_sem.at[2])
+    own_wedge.start()
     sends = []
     for k in range(1, tomo_axis):
         target = lax.rem(me_t + k, tomo_axis)
         one = copy(m_ref.at[target], mine, (target, me_c), s1.at[k], r1.at[k])
         one.start()
         sends.append(one)
+    for k in range(1, tomo_axis):
+        one = wedge_copy(k, me_t, (lax.rem(me_t + k, tomo_axis), me_c))
+        one.start()
+        sends.append(one)
+    run(1, count, lambda k: code_copy(k, mine, device_of(lax.rem(mine + k, count))).start())
     for k in range(tomo_axis):
         source = lax.rem(me_t + tomo_axis - k, tomo_axis)
         slot = source * cls_axis + me_c
@@ -183,30 +246,51 @@
         for d in range(x_axis):
             slot = source * cls_axis + x_source(d) * 2 + 1 - core
             copy(out_ref.at[slot], slot, (me_t, sibling), sc.at[d, k], rc.at[d, k]).wait_recv()
+    own_codes.wait()
+    own_wedge.wait()
+    for k in range(1, tomo_axis):
+        source = lax.rem(me_t + tomo_axis - k, tomo_axis)
+        wedge_copy(k, source, (source, me_c)).wait_recv()
+
+    def code_arrived(k):
+        source = lax.rem(mine + count - k, count)
+        code_copy(k, source, device_of(source)).wait_recv()
+
+    run(1, count, code_arrived)
+    run(1, count, lambda k: code_copy(k, mine, device_of(lax.rem(mine + k, count))).wait_send())
     for one in sends:
         one.wait_send()
 
 
-def exchange(chunks, tomo_axis, cls_axis):
+def exchange(chunks, code_rows, wedge_own, tomo_axis, cls_axis):
+    count = tomo_axis * cls_axis
     x_axis = cls_axis // 2
     dma = pltpu.SemaphoreType.DMA
     return pl.pallas_call(
         functools.partial(exchange_kernel, tomo_axis, cls_axis),
-        out_shape=jax.ShapeDtypeStruct((tomo_axis * cls_axis,) + chunks.shape[1:], BF16),
-        in_specs=[pl.BlockSpec(memory_space=pl.ANY)],
-        out_specs=pl.BlockSpec(memory_space=pl.ANY),
+        out_shape=(
+            jax.ShapeDtypeStruct((count,) + chunks.shape[1:], BF16),
+            jax.ShapeDtypeStruct((count,) + code_rows.shape, jnp.int32),
+            jax.ShapeDtypeStruct((tomo_axis,) + wedge_own.shape, BF16),
+        ),
+        in_specs=[pl.BlockSpec(memory_space=pl.ANY)] * 3,
+        out_specs=(pl.BlockSpec(memory_space=pl.ANY),) * 3,
         scratch_shapes=[
-            dma,
+            dma((3,)),
             dma((tomo_axis,)),
             dma((tomo_axis,)),
             dma((x_axis, tomo_axis)),
             dma((x_axis, tomo_axis)),
             dma((x_axis, tomo_axis)),
             dma((x_axis, tomo_axis)),
+            dma((count,)),
+            dma((count,)),
+            dma((tomo_axis,)),
+            dma((tomo_axis,)),
         ],
         compiler_params=pltpu.CompilerParams(collective_id=1, has_side_effects=True),
         name="exchange",
-    )(chunks)
+    )(chunks, code_rows, wedge_own)
 
 
 def score_kernel(place_ref, slots_ref, refs_ref, wedge_ref, codes_ref, out_ref, acc, pen):
@@ -477,11 +561,6 @@
         ],
         axis=1,
     )
-    codes = lax.all_gather(code_rows, ("tomo", "cls"), axis=0, tiled=True)
-    wedge_rows = lax.all_gather(
-        wedge.reshape(tomo_count, KB * KB).astype(BF16), "tomo", axis=0, tiled=True
-    )
-
     local_hot = (
         (tomogram - here * tomo_count)[:, None] == jnp.arange(tomo_count, dtype=jnp.int32)[None, :]
     ).astype(F32)
@@ -490,7 +569,10 @@
     mask_rows = jnp.tile(own_masks.reshape(KB * part_count, KB), (1, LANES // KB))
 
     chunks = spectra_chunks(particles, mask_rows, tomo_axis)
-    slots = exchange(chunks, tomo_axis, cls_axis)
+    wedge_own = wedge.reshape(-1, LANES).astype(BF16)
+    slots, codes, wedge_rows = exchange(chunks, code_rows, wedge_own, tomo_axis, cls_axis)
+    codes = codes.reshape(-1, LANES)
+    wedge_rows = wedge_rows.reshape(-1, KB * KB)
     slots = slots.reshape(-1, slots.shape[-1])
 
     total_tomos = wedge_rows.shape[0]

time: 197 us -> 131 us (0.66)
  blocking collectives: 76.7 us -> 0 us
  Pallas kernels: 109 us -> 118 us
    all_gather x2 -> x0, blocking collectives: 76.7 us -> none  [the longest x1 44.4 us: body(): codes = lax.all_gather(code_rows, ('tomo', 'cls'), axis=0, tiled=True)]
    pallas_call x1, Pallas kernels: 34.2 us -> 42.6 us  [exchange(): pl.pallas_call(functools.partial(exchange_kernel, tomo_axis, cls_axis), o...]
where the time goes in v2:
time: 131 us
  Pallas kernels  118 us (90%)
  local copies, waits for them, and re-layouts  7.85 us (6%)
  other arithmetic  4.27 us (3%)
    pallas_call x1, Pallas kernels, exchange(): pl.pallas_call(functools.partial(exchange_kernel, tomo_axis, cls_axis), o...  42.6 us
    pallas_call x1, Pallas kernels, spectra_chunks(): pl.pallas_call(functools.partial(dft_kernel, blocks, half), grid=(tiles,)...  33.7 us
    pallas_call x1, Pallas kernels, weights(): pl.pallas_call(functools.partial(weights_kernel, tomo_axis, cls_axis), ou...  24.4 us
    pallas_call x1, Pallas kernels, sums(): pl.pallas_call(sums_kernel, grid_spec=pltpu.PrefetchScalarGridSpec(num_sc...  9.81 us
    pallas_call x1, Pallas kernels, scores(): pl.pallas_call(score_kernel, grid_spec=pltpu.PrefetchScalarGridSpec(num_s...  7.28 us

profile of v2, /device:TPU:0, one launch (start us, length us, event | category | flops | bytes accessed | tf_op | source)
XLA Modules:
  0.0 130.9 jit_solution(9679143154581327930)
XLA Ops:
  0.6 0.7 pad_add_fusion.place_ref
  1.3 0.7 broadcast_subtract_fusion
  2.0 0.7 broadcast_multiply_fusion
  2.7 0.1 copy.20
  2.8 1.3 broadcast_in_dim.27.noise_ref
  4.1 0.7 copy.21
  4.8 0.8 broadcast_add_fusion
  5.7 0.7 add_add_fusion.code_ref
  6.3 0.8 convert_element_type.18
  7.2 0.1 convert_element_type.13
  7.3 0.7 convert_element_type.15.wedge_ref
  8.0 0.1 dot_general.8
  8.1 0.2 convolution_bitcast_fusion
  8.4 0.7 copy.19.mask_ref
  9.2 33.7 %dft.1.m_ref = bf16[8,16,4096]{2,1,0:T(8,128)(2,1)} custom-call(bf16[512,4096]{1,0:T(8,128)(2,1)} %bitcast.27, bf16[4096,2048]{1,0:T(8,128)(2,1)} %constant.33.clone.th_ref, bf16[4096,2048]{1,0:T(8,128)(2,1)} %constant.34.clone.tl_ref, bf16[512,512]{1,0:T(8,128)(2,1)} %constant.35.clone.wh_ref, bf16[512,512]{1,0:T(8,128)(2,1)} %constant.36.clone.wl_ref, ...), custom_call_target="tpu_custom_call" | custom-call | tf_op jit(solution)/shard_map/dft/pallas_call | solution.py:95
  42.9 42.6 %exchange.1 = (bf16[32,16,4096]{2,1,0:T(8,128)(2,1)}, s32[32,8,128]{2,1,0:T(8,128)}, bf16[8,32,128]{2,1,0:T(8,128)(2,1)}) custom-call(bf16[8,16,4096]{2,1,0:T(8,128)(2,1)} %dft.1.m_ref, s32[8,128]{1,0:T(8,128)} %add_add_fusion.code_ref, bf16[32,128]{1,0:T(8,128)(2,1)} %convert_element_type.15.wedge_ref), custom_call_target="tpu_custom_call" | custom-call | tf_op jit(solution)/shard_map/exchange/pallas_call | solution.py:269
  85.5 0.9 reshape.60
  86.4 0.6 constant_dynamic-slice_fusion.wedge_ref
  87.0 0.1 broadcast_in_dim.12
  87.2 0.9 reshape.61.wedge_ref
  88.1 7.3 %scores.1 = f32[256,128]{1,0:T(8,128)} custom-call(s32[2]{0:T(128)} %pad_add_fusion.place_ref, bf16[512,4096]{1,0:T(8,128)(2,1)} %bitcast.25, bf16[128,65536]{1,0:T(8,128)(2,1)} %bitcast.24, bf16[32,1024]{1,0:T(8,128)(2,1)} %reshape.61.wedge_ref, s32[256,128]{1,0:T(8,128)} %bitcast.28), custom_call_target="tpu_custom_call" | custom-call | tf_op jit(solution)/shard_map/scores/pallas_call | solution.py:352
  95.3 24.4 %weights.1 = (f32[8,128]{1,0:T(8,128)}, f32[32,8,128]{2,1,0:T(8,128)}) custom-call(f32[32,8,128]{2,1,0:T(8,128)} %bitcast.30, f32[8,128]{1,0:T(8,128)} %broadcast_in_dim.27.noise_ref), custom_call_target="tpu_custom_call" | custom-call | tf_op jit(solution)/shard_map/weights/pallas_call | solution.py:459
  119.8 9.8 %sums.1 = (f32[128,8192]{1,0:T(8,128)}, f32[128,128]{1,0:T(8,128)}) custom-call(s32[2]{0:T(128)} %pad_add_fusion.place_ref, bf16[512,4096]{1,0:T(8,128)(2,1)} %bitcast.26, s32[256,128]{1,0:T(8,128)} %bitcast.29, f32[256,128]{1,0:T(8,128)} %bitcast.33, bf16[32,128]{1,0:T(8,128)(2,1)} %constant_dynamic-slice_fusion.wedge_ref), custom_call_target="tpu_custom_call" | custom-call | tf_op jit(solution)/shard_map/sums/pallas_call | solution.py:507
  129.6 1.3 copy.26
  (8 shorter events, 0.3 us)

commit v3 on v1

--- a/solution.py
+++ b/solution.py
@@ -15,6 +15,7 @@
 ROT = 8
 CAND = 4
 LANES = 128
+GROUPS = 4
 MESH = pl.DeviceIdType.MESH
 BF16 = jnp.bfloat16
 F32 = jnp.float32
@@ -63,8 +64,149 @@
     return jnp.dot(a, b, preferred_element_type=F32)
 
 
-def dft_kernel(blocks, half, x_ref, th_ref, tl_ref, wh_ref, wl_ref, mask_ref, out_ref):
+def spectra_kernel(
+    tomo_axis,
+    cls_axis,
+    x_ref,
+    th_ref,
+    tl_ref,
+    wh_ref,
+    wl_ref,
+    mask_ref,
+    code_ref,
+    wedge_ref,
+    out_ref,
+    codes_ref,
+    wedges_ref,
+    m_ref,
+    local_sem,
+    s1,
+    r1,
+    sx,
+    rx,
+    sc,
+    rc,
+    sk,
+    rk,
+    sw,
+    rw,
+):
     tile = pl.program_id(0)
+    count = tomo_axis * cls_axis
+    blocks = tomo_axis // 2
+    half = KB // blocks // 2
+    per_group = KB * KB // LANES // GROUPS
+    lanes = per_group * LANES
+    me_t, me_c = lax.axis_index("tomo"), lax.axis_index("cls")
+    mine = me_t * cls_axis + me_c
+    x_axis = cls_axis // 2
+    xi, core = me_c // 2, me_c % 2
+    sibling = (me_t, xi * 2 + 1 - core)
+
+    def x_peer(d):
+        return (me_t, lax.rem(xi + d, x_axis) * 2 + core)
+
+    def x_source(d):
+        return lax.rem(xi + x_axis - d, x_axis)
+
+    def tomo_source(k):
+        return lax.rem(me_t + tomo_axis - k, tomo_axis)
+
+    def remote(src, dst, send, recv, device):
+        return pltpu.make_async_remote_copy(
+            src_ref=src,
+            dst_ref=dst,
+            send_sem=send,
+            recv_sem=recv,
+            device_id=device,
+            device_id_type=MESH,
+        )
+
+    def device_of(index):
+        return (index // cls_axis, lax.rem(index, cls_axis))
+
+    def code_copy(k, slot, device):
+        return remote(code_ref, codes_ref.at[slot], sk.at[k], rk.at[k], device)
+
+    def wedge_copy(k, slot, device):
+        return remote(wedge_ref, wedges_ref.at[slot], sw.at[k], rw.at[k], device)
+
+    def first(g, k):
+        target = lax.rem(me_t + k, tomo_axis)
+        return remote(
+            m_ref.at[g, target], out_ref.at[g, mine], s1.at[g, k], r1.at[g, k], (target, me_c)
+        )
+
+    def first_arrived(g, k):
+        slot = tomo_source(k) * cls_axis + me_c
+        return remote(
+            m_ref.at[g, 0], out_ref.at[g, slot], s1.at[g, k], r1.at[g, k], (tomo_source(k), me_c)
+        )
+
+    def across(g, d, k, slot):
+        here = out_ref.at[g, slot]
+        return remote(here, here, sx.at[g, d, k], rx.at[g, d, k], x_peer(d))
+
+    def over(g, d, k, slot):
+        here = out_ref.at[g, slot]
+        return remote(here, here, sc.at[g, d, k], rc.at[g, d, k], sibling)
+
+    def own_copy(g):
+        return pltpu.make_async_copy(m_ref.at[g, me_t], out_ref.at[g, mine], local_sem.at[g])
+
+    def own_small():
+        return (
+            pltpu.make_async_copy(code_ref, codes_ref.at[mine], local_sem.at[GROUPS]),
+            pltpu.make_async_copy(wedge_ref, wedges_ref.at[me_t], local_sem.at[GROUPS + 1]),
+        )
+
+    def run(low, high, step):
+        def loop(k, carry):
+            step(k)
+            return carry
+
+        lax.fori_loop(low, high, loop, 0)
+
+    def send(g):
+        own_copy(g).start()
+        for k in range(1, tomo_axis):
+            first(g, k).start()
+
+    def forward(g):
+        for k in range(tomo_axis):
+            slot = tomo_source(k) * cls_axis + me_c
+            if k == 0:
+                own_copy(g).wait()
+            else:
+                first_arrived(g, k).wait_recv()
+            for d in range(1, x_axis):
+                across(g, d, k, slot).start()
+            over(g, 0, k, slot).start()
+
+    def share(g):
+        for k in range(tomo_axis):
+            for d in range(1, x_axis):
+                slot = tomo_source(k) * cls_axis + x_source(d) * 2 + core
+                across(g, d, k, slot).wait_recv()
+                over(g, d, k, slot).start()
+
+    @pl.when(tile == 0)
+    def _():
+        barrier = pltpu.get_barrier_semaphore()
+        run(
+            1,
+            count,
+            lambda k: pl.semaphore_signal(
+                barrier, inc=1, device_id=device_of(lax.rem(mine + k, count)), device_id_type=MESH
+            ),
+        )
+        pl.semaphore_wait(barrier, count - 1)
+        for one in own_small():
+            one.start()
+        for k in range(1, tomo_axis):
+            wedge_copy(k, me_t, (lax.rem(me_t + k, tomo_axis), me_c)).start()
+        run(1, count, lambda k: code_copy(k, mine, device_of(lax.rem(mine + k, count))).start())
+
     values = x_ref[...]
     plane = dot(values, th_ref[...]) + dot(values, tl_ref[...])
     high = plane.astype(BF16)
@@ -74,28 +216,82 @@
     mask = mask_ref[...]
     real = (wide[:rows, :LANES] - wide[rows:, LANES:]) * mask
     imag = (wide[:rows, LANES:] + wide[rows:, :LANES]) * mask
-    group = rows // (blocks * half)
+    height = rows // (blocks * half)
+    at = tile // per_group
+    offset = lax.rem(tile, per_group) * LANES
     for a, part in enumerate((real.astype(BF16), imag.astype(BF16))):
         for block in range(blocks):
             for k in range(half):
-                start = (block * half + k) * group
-                column = pl.multiple_of(k * KB * KB + tile * LANES, LANES)
-                out_ref[a * blocks + block, :, pl.ds(column, LANES)] = part[start : start + group]
-
-
-def spectra_chunks(particles, mask_rows, tomo_axis):
+                start = (block * half + k) * height
+                column = pl.multiple_of(k * lanes + offset, LANES)
+                m_ref[at, a * blocks + block, :, pl.ds(column, LANES)] = part[
+                    start : start + height
+                ]
+
+    for g in range(GROUPS):
+
+        @pl.when(tile == (g + 1) * per_group - 1)
+        def _(g=g):
+            send(g)
+            if g >= 1:
+                forward(g - 1)
+            if g >= 2:
+                share(g - 2)
+
+    @pl.when(tile == GROUPS * per_group - 1)
+    def _():
+        if GROUPS >= 2:
+            share(GROUPS - 2)
+        forward(GROUPS - 1)
+        share(GROUPS - 1)
+        for g in range(GROUPS):
+            for k in range(tomo_axis):
+                for d in range(x_axis):
+                    slot = tomo_source(k) * cls_axis + x_source(d) * 2 + 1 - core
+                    over(g, d, k, slot).wait_recv()
+        for one in own_small():
+            one.wait()
+        for k in range(1, tomo_axis):
+            wedge_copy(k, tomo_source(k), (tomo_source(k), me_c)).wait_recv()
+
+        def code_arrived(k):
+            source = lax.rem(mine + count - k, count)
+            code_copy(k, source, device_of(source)).wait_recv()
+
+        run(1, count, code_arrived)
+        run(1, count, lambda k: code_copy(k, mine, device_of(lax.rem(mine + k, count))).wait_send())
+        for k in range(1, tomo_axis):
+            wedge_copy(k, me_t, (lax.rem(me_t + k, tomo_axis), me_c)).wait_send()
+        for g in range(GROUPS):
+            for k in range(tomo_axis):
+                if k:
+                    first(g, k).wait_send()
+                for d in range(x_axis):
+                    slot = tomo_source(k) * cls_axis + x_source(d) * 2 + core
+                    if d:
+                        across(g, d, k, tomo_source(k) * cls_axis + me_c).wait_send()
+                    over(g, d, k, slot).wait_send()
+
+
+def spectra_slots(particles, mask_rows, code_rows, wedge_own, tomo_axis, cls_axis):
     part_count, length, plane_size = particles.shape
-    blocks = tomo_axis // 2
-    half = KB // blocks // 2
-    width = half * KB * KB
+    count = tomo_axis * cls_axis
+    x_axis = cls_axis // 2
+    half = KB // tomo_axis
+    piece = half * KB * KB // GROUPS
     th, tl = plane_tables(length)
     wh, wl = depth_tables(length, part_count, tomo_axis)
     tiles = KB * KB // LANES
+    dma = pltpu.SemaphoreType.DMA
     whole = lambda shape: pl.BlockSpec(shape, lambda j: (0,) * len(shape))
     return pl.pallas_call(
-        functools.partial(dft_kernel, blocks, half),
+        functools.partial(spectra_kernel, tomo_axis, cls_axis),
         grid=(tiles,),
-        out_shape=jax.ShapeDtypeStruct((tomo_axis, 2 * part_count, width), BF16),
+        out_shape=(
+            jax.ShapeDtypeStruct((GROUPS, count, 2 * part_count, piece), BF16),
+            jax.ShapeDtypeStruct((count,) + code_rows.shape, jnp.int32),
+            jax.ShapeDtypeStruct((tomo_axis,) + wedge_own.shape, BF16),
+        ),
         in_specs=[
             whole((part_count * length, plane_size)),
             pl.BlockSpec((plane_size, 2 * LANES), lambda j: (0, j)),
@@ -103,10 +299,28 @@
             whole(wh.shape),
             whole(wl.shape),
             whole(mask_rows.shape),
+            pl.BlockSpec(memory_space=pl.ANY),
+            pl.BlockSpec(memory_space=pl.ANY),
         ],
-        out_specs=whole((tomo_axis, 2 * part_count, width)),
-        compiler_params=pltpu.CompilerParams(vmem_limit_bytes=VMEM_LIMIT),
-        name="dft",
+        out_specs=(pl.BlockSpec(memory_space=pl.ANY),) * 3,
+        scratch_shapes=[
+            pltpu.VMEM((GROUPS, tomo_axis, 2 * part_count, piece), BF16),
+            dma((GROUPS + 2,)),
+            dma((GROUPS, tomo_axis)),
+            dma((GROUPS, tomo_axis)),
+            dma((GROUPS, x_axis, tomo_axis)),
+            dma((GROUPS, x_axis, tomo_axis)),
+            dma((GROUPS, x_axis, tomo_axis)),
+            dma((GROUPS, x_axis, tomo_axis)),
+            dma((count,)),
+            dma((count,)),
+            dma((tomo_axis,)),
+            dma((tomo_axis,)),
+        ],
+        compiler_params=pltpu.CompilerParams(
+            collective_id=1, has_side_effects=True, vmem_limit_bytes=VMEM_LIMIT
+        ),
+        name="spectra",
     )(
         particles.reshape(part_count * length, plane_size),
         jnp.asarray(th),
@@ -114,107 +328,28 @@
         jnp.asarray(wh),
         jnp.asarray(wl),
         mask_rows,
-    )
-
-
-def exchange_kernel(tomo_axis, cls_axis, m_ref, out_ref, local_sem, s1, r1, sx, rx, sc, rc):
-    me_t, me_c = lax.axis_index("tomo"), lax.axis_index("cls")
-    x_axis = cls_axis // 2
-    xi, core = me_c // 2, me_c % 2
-    sibling = xi * 2 + 1 - core
-
-    def x_peer(d):
-        return lax.rem(xi + d, x_axis) * 2 + core
-
-    def x_source(d):
-        return lax.rem(xi + x_axis - d, x_axis)
-
-    def copy(src, slot, device, send, recv):
-        return pltpu.make_async_remote_copy(
-            src_ref=src,
-            dst_ref=out_ref.at[slot],
-            send_sem=send,
-            recv_sem=recv,
-            device_id=device,
-            device_id_type=MESH,
-        )
-
-    barrier = pltpu.get_barrier_semaphore()
-    peers = [(lax.rem(me_t + k, tomo_axis), me_c) for k in range(1, tomo_axis)]
-    peers += [(me_t, x_peer(d)) for d in range(1, x_axis)]
-    peers += [(me_t, sibling)]
-    for device in peers:
-        pl.semaphore_signal(barrier, inc=1, device_id=device, device_id_type=MESH)
-    pl.semaphore_wait(barrier, len(peers))
-
-    mine = me_t * cls_axis + me_c
-    own = pltpu.make_async_copy(m_ref.at[me_t], out_ref.at[mine], local_sem)
-    own.start()
-    sends = []
-    for k in range(1, tomo_axis):
-        target = lax.rem(me_t + k, tomo_axis)
-        one = copy(m_ref.at[target], mine, (target, me_c), s1.at[k], r1.at[k])
-        one.start()
-        sends.append(one)
-    for k in range(tomo_axis):
-        source = lax.rem(me_t + tomo_axis - k, tomo_axis)
-        slot = source * cls_axis + me_c
-        if k == 0:
-            own.wait()
-        else:
-            copy(m_ref.at[0], slot, (source, me_c), s1.at[k], r1.at[k]).wait_recv()
-        for d in range(1, x_axis):
-            one = copy(out_ref.at[slot], slot, (me_t, x_peer(d)), sx.at[d, k], rx.at[d, k])
-            one.start()
-            sends.append(one)
-        one = copy(out_ref.at[slot], slot, (me_t, sibling), sc.at[0, k], rc.at[0, k])
-        one.start()
-        sends.append(one)
-    for k in range(tomo_axis):
-        source = lax.rem(me_t + tomo_axis - k, tomo_axis)
-        for d in range(1, x_axis):
-            slot = source * cls_axis + x_source(d) * 2 + core
-            copy(out_ref.at[slot], slot, (me_t, x_peer(d)), sx.at[d, k], rx.at[d, k]).wait_recv()
-            one = copy(out_ref.at[slot], slot, (me_t, sibling), sc.at[d, k], rc.at[d, k])
-            one.start()
-            sends.append(one)
-    for k in range(tomo_axis):
-        source = lax.rem(me_t + tomo_axis - k, tomo_axis)
-        for d in range(x_axis):
-            slot = source * cls_axis + x_source(d) * 2 + 1 - core
-            copy(out_ref.at[slot], slot, (me_t, sibling), sc.at[d, k], rc.at[d, k]).wait_recv()
-    for one in sends:
-        one.wait_send()
-
-
-def exchange(chunks, tomo_axis, cls_axis):
-    x_axis = cls_axis // 2
-    dma = pltpu.SemaphoreType.DMA
-    return pl.pallas_call(
-        functools.partial(exchange_kernel, tomo_axis, cls_axis),
-        out_shape=jax.ShapeDtypeStruct((tomo_axis * cls_axis,) + chunks.shape[1:], BF16),
-        in_specs=[pl.BlockSpec(memory_space=pl.ANY)],
-        out_specs=pl.BlockSpec(memory_space=pl.ANY),
-        scratch_shapes=[
-            dma,
-            dma((tomo_axis,)),
-            dma((tomo_axis,)),
-            dma((x_axis, tomo_axis)),
-            dma((x_axis, tomo_axis)),
-            dma((x_axis, tomo_axis)),
-            dma((x_axis, tomo_axis)),
-        ],
-        compiler_params=pltpu.CompilerParams(collective_id=1, has_side_effects=True),
-        name="exchange",
-    )(chunks)
+        code_rows,
+        wedge_own,
+    )
 
 
 def score_kernel(place_ref, slots_ref, refs_ref, wedge_ref, codes_ref, out_ref, acc, pen):
     h = pl.program_id(0)
     refs = refs_ref[...]
-    products = lax.dot_general(
-        slots_ref[...], refs, (((1,), (1,)), ((), ())), preferred_element_type=F32
-    )
+    products = None
+    lanes = KB * KB // GROUPS
+    for g in range(GROUPS):
+        columns = jnp.concatenate(
+            [
+                refs[:, k * KB * KB + g * lanes : k * KB * KB + (g + 1) * lanes]
+                for k in range(refs.shape[1] // (KB * KB))
+            ],
+            axis=1,
+        )
+        term = lax.dot_general(
+            slots_ref[g], columns, (((1,), (1,)), ((), ())), preferred_element_type=F32
+        )
+        products = term if products is None else products + term
     rows, wide = products.shape
     paired = products.reshape(rows // 16, 16, wide)
     inner = jnp.where(h == 0, paired[:, :8], paired[:, 8:]).reshape(rows // 2, wide)
@@ -261,7 +396,7 @@
 
 
 def scores(place, slots, refs, wedge_block, codes):
-    rows, width = slots.shape
+    rows, width = slots.shape[1], slots.shape[2] * GROUPS
     tomos = wedge_block.shape[0]
     depth = wedge_block.shape[1] // 2
     wide = refs.shape[0]
@@ -271,7 +406,7 @@
             num_scalar_prefetch=1,
             grid=(2,),
             in_specs=[
-                pl.BlockSpec((rows, width), lambda h, place: (0, 0)),
+                pl.BlockSpec(slots.shape, lambda h, place: (0, 0, 0)),
                 pl.BlockSpec((wide, width), lambda h, place: (0, 2 * place[0] + h)),
                 pl.BlockSpec((tomos, depth), lambda h, place: (0, h)),
                 pl.BlockSpec(codes.shape, lambda h, place: (0, 0)),
@@ -413,26 +548,29 @@
         masks = dot(hot.astype(F32).astype(BF16), wedge_ref[...]).astype(BF16)
         wsum_ref[...] = dot(total.T.astype(BF16), masks)
 
-    class_ref[...] = dot(table[h], slots_ref[...])
+    lanes = KB * KB // GROUPS
+    result = dot(table[h], slots_ref[0])
+    for k in range(result.shape[1] // lanes):
+        column = pl.multiple_of(k * KB * KB + tile * lanes, lanes)
+        class_ref[:, pl.ds(column, lanes)] = result[:, k * lanes : (k + 1) * lanes]
 
 
 def sums(place, slots, codes, all_weights, wedge_columns, wide):
-    rows, width = slots.shape
-    tiles = 2
-    step = width // tiles
+    rows, step = slots.shape[1:]
+    width = step * GROUPS
     return pl.pallas_call(
         sums_kernel,
         grid_spec=pltpu.PrefetchScalarGridSpec(
             num_scalar_prefetch=1,
-            grid=(2, tiles),
+            grid=(2, GROUPS),
             in_specs=[
-                pl.BlockSpec((rows, step), lambda h, i, place: (0, i)),
+                pl.BlockSpec((1, rows, step), lambda h, i, place: (i, 0, 0)),
                 pl.BlockSpec(codes.shape, lambda h, i, place: (0, 0)),
                 pl.BlockSpec(all_weights.shape, lambda h, i, place: (0, 0)),
                 pl.BlockSpec(wedge_columns.shape, lambda h, i, place: (0, 0)),
             ],
             out_specs=[
-                pl.BlockSpec((wide, step), lambda h, i, place: (0, h * tiles + i)),
+                pl.BlockSpec((wide, width), lambda h, i, place: (0, h)),
                 pl.BlockSpec((wide, wedge_columns.shape[1]), lambda h, i, place: (0, 0)),
             ],
             scratch_shapes=[pltpu.VMEM((2, wide, rows), BF16)],
@@ -477,11 +615,6 @@
         ],
         axis=1,
     )
-    codes = lax.all_gather(code_rows, ("tomo", "cls"), axis=0, tiled=True)
-    wedge_rows = lax.all_gather(
-        wedge.reshape(tomo_count, KB * KB).astype(BF16), "tomo", axis=0, tiled=True
-    )
-
     local_hot = (
         (tomogram - here * tomo_count)[:, None] == jnp.arange(tomo_count, dtype=jnp.int32)[None, :]
     ).astype(F32)
@@ -489,9 +622,13 @@
     own_masks = own_masks.reshape(part_count, blocks, 2, half, KB).transpose(1, 3, 2, 0, 4)
     mask_rows = jnp.tile(own_masks.reshape(KB * part_count, KB), (1, LANES // KB))
 
-    chunks = spectra_chunks(particles, mask_rows, tomo_axis)
-    slots = exchange(chunks, tomo_axis, cls_axis)
-    slots = slots.reshape(-1, slots.shape[-1])
+    wedge_own = wedge.reshape(-1, LANES).astype(BF16)
+    slots, codes, wedge_rows = spectra_slots(
+        particles, mask_rows, code_rows, wedge_own, tomo_axis, cls_axis
+    )
+    codes = codes.reshape(-1, LANES)
+    wedge_rows = wedge_rows.reshape(-1, KB * KB)
+    slots = slots.reshape(GROUPS, -1, slots.shape[-1])
 
     total_tomos = wedge_rows.shape[0]
     wedge_block = lax.dynamic_slice_in_dim(

time: 197 us -> 110 us (0.56)
  blocking collectives: 76.7 us -> 0 us
  Pallas kernels: 109 us -> 96.5 us
    all_gather x2 -> x0, blocking collectives: 76.7 us -> none  [the longest x1 44.4 us: body(): codes = lax.all_gather(code_rows, ('tomo', 'cls'), axis=0, tiled=True)]
    pallas_call x1, Pallas kernels: 24.1 us -> 16 us  [weights(): pl.pallas_call(functools.partial(weights_kernel, tomo_axis, cls_axis), ou...]
    pallas_call x2 -> x1, Pallas kernels: 67.9 us -> 61 us  [spectra_slots(): pl.pallas_call(functools.partial(spectra_kernel, tomo_axis, cls_axis), gr...]
    pallas_call x1, Pallas kernels: 9.82 us -> 12.2 us  [sums(): pl.pallas_call(sums_kernel, grid_spec=pltpu.PrefetchScalarGridSpec(num_sc...]
where the time goes in v3:
time: 110 us
  Pallas kernels  96.5 us (88%)
  local copies, waits for them, and re-layouts  7.86 us (7%)
  other arithmetic  4.27 us (4%)
    pallas_call x1, Pallas kernels, spectra_slots(): pl.pallas_call(functools.partial(spectra_kernel, tomo_axis, cls_axis), gr...  61 us
    pallas_call x1, Pallas kernels, weights(): pl.pallas_call(functools.partial(weights_kernel, tomo_axis, cls_axis), ou...  16 us
    pallas_call x1, Pallas kernels, sums(): pl.pallas_call(sums_kernel, grid_spec=pltpu.PrefetchScalarGridSpec(num_sc...  12.2 us
    pallas_call x1, Pallas kernels, scores(): pl.pallas_call(score_kernel, grid_spec=pltpu.PrefetchScalarGridSpec(num_s...  7.28 us

profile of v3, /device:TPU:0, one launch (start us, length us, event | category | flops | bytes accessed | tf_op | source)
XLA Modules:
  0.0 109.6 jit_solution(13437100146818690770)
XLA Ops:
  0.6 0.7 pad_add_fusion.place_ref
  1.3 0.7 broadcast_subtract_fusion
  2.0 0.7 broadcast_multiply_fusion
  2.7 0.1 copy.19
  2.8 1.3 %broadcast_in_dim.27.noise_ref = f32[8,128]{1,0:T(8,128)} broadcast(f32[8]{0:T(128)} %param.12), dimensions={0} | broadcast | bytes 4128 | tf_op jit(solution)/shard_map/broadcast_in_dim | solution.py:642
  4.1 0.7 copy.20
  4.8 0.8 broadcast_add_fusion
  5.6 0.1 add.26
  5.7 0.7 add_add_fusion.code_ref
  6.3 0.8 convert_element_type.18
  7.2 0.1 convert_element_type.13
  7.3 0.7 convert_element_type.15.wedge_ref
  8.0 0.1 dot_general.8
  8.1 0.2 convolution_bitcast_fusion
  8.4 0.8 copy.21.mask_ref
  9.2 61.0 %spectra.1 = (bf16[4,32,16,1024]{3,2,1,0:T(8,128)(2,1)}, s32[32,8,128]{2,1,0:T(8,128)}, bf16[8,32,128]{2,1,0:T(8,128)(2,1)}) custom-call(bf16[512,4096]{1,0:T(8,128)(2,1)} %bitcast.27, bf16[4096,2048]{1,0:T(8,128)(2,1)} %constant.33.clone.th_ref, bf16[4096,2048]{1,0:T(8,128)(2,1)} %constant.34.clone.tl_ref, bf16[512,512]{1,0:T(8,128)(2,1)} %constant.35.clone.wh_ref, ...), custom_call_target="tpu_custom_call" | custom-call | tf_op jit(solution)/shard_map/spectra/pallas_call | solution.py:287
  70.2 0.9 reshape.60
  71.0 0.6 constant_dynamic-slice_fusion.wedge_ref
  71.7 0.1 broadcast_in_dim.12
  71.9 0.9 reshape.61.wedge_ref
  72.8 7.3 %scores.1 = f32[256,128]{1,0:T(8,128)} custom-call(s32[2]{0:T(128)} %pad_add_fusion.place_ref, bf16[4,512,1024]{2,1,0:T(8,128)(2,1)} %bitcast.25, bf16[128,65536]{1,0:T(8,128)(2,1)} %bitcast.24, bf16[32,1024]{1,0:T(8,128)(2,1)} %reshape.61.wedge_ref, s32[256,128]{1,0:T(8,128)} %bitcast.28), custom_call_target="tpu_custom_call" | custom-call | tf_op jit(solution)/shard_map/scores/pallas_call | solution.py:403
  80.0 16.0 %weights.1 = (f32[8,128]{1,0:T(8,128)}, f32[32,8,128]{2,1,0:T(8,128)}) custom-call(f32[32,8,128]{2,1,0:T(8,128)} %bitcast.30, f32[8,128]{1,0:T(8,128)} %broadcast_in_dim.27.noise_ref), custom_call_target="tpu_custom_call" | custom-call | tf_op jit(solution)/shard_map/weights/pallas_call | solution.py:510
  96.1 12.2 %sums.1 = (f32[128,8192]{1,0:T(8,128)}, f32[128,128]{1,0:T(8,128)}) custom-call(s32[2]{0:T(128)} %pad_add_fusion.place_ref, bf16[4,512,1024]{2,1,0:T(8,128)(2,1)} %bitcast.26, s32[256,128]{1,0:T(8,128)} %bitcast.29, f32[256,128]{1,0:T(8,128)} %bitcast.33, bf16[32,128]{1,0:T(8,128)(2,1)} %constant_dynamic-slice_fusion.wedge_ref), custom_call_target="tpu_custom_call" | custom-call | tf_op jit(solution)/shard_map/sums/pallas_call | solution.py:561
  108.3 1.3 %copy.26 = f32[8,32]{1,0:T(8,128)} copy(f32[8,32]{1,0:T(8,128)} %bitcast.35) | data formatting | bytes 2048
  (7 shorter events, 0.2 us)

commit v4 on v3

--- a/solution.py
+++ b/solution.py
@@ -523,11 +523,11 @@
 
 
 def sums_kernel(place_ref, slots_ref, codes_ref, weights_ref, wedge_ref, class_ref, wsum_ref, table):
-    h, tile = pl.program_id(0), pl.program_id(1)
+    k_block, h = pl.program_id(0), pl.program_id(1)
     particles = codes_ref.shape[0]
     wide = class_ref.shape[0]
 
-    @pl.when((h == 0) & (tile == 0))
+    @pl.when((h == 0) & (k_block == 0))
     def _():
         local = codes_ref[...] - place_ref[1]
         value = weights_ref[...]
@@ -548,29 +548,29 @@
         masks = dot(hot.astype(F32).astype(BF16), wedge_ref[...]).astype(BF16)
         wsum_ref[...] = dot(total.T.astype(BF16), masks)
 
-    lanes = KB * KB // GROUPS
-    result = dot(table[h], slots_ref[0])
-    for k in range(result.shape[1] // lanes):
-        column = pl.multiple_of(k * KB * KB + tile * lanes, lanes)
-        class_ref[:, pl.ds(column, lanes)] = result[:, k * lanes : (k + 1) * lanes]
+    lanes = slots_ref.shape[2]
+    for g in range(GROUPS):
+        class_ref[:, g * lanes : (g + 1) * lanes] = dot(table[h], slots_ref[g])
 
 
 def sums(place, slots, codes, all_weights, wedge_columns, wide):
     rows, step = slots.shape[1:]
     width = step * GROUPS
+    lanes = KB * KB // GROUPS
+    half = step // lanes
     return pl.pallas_call(
         sums_kernel,
         grid_spec=pltpu.PrefetchScalarGridSpec(
             num_scalar_prefetch=1,
-            grid=(2, GROUPS),
+            grid=(half, 2),
             in_specs=[
-                pl.BlockSpec((1, rows, step), lambda h, i, place: (i, 0, 0)),
+                pl.BlockSpec((GROUPS, rows, lanes), lambda i, h, place: (0, 0, i)),
                 pl.BlockSpec(codes.shape, lambda h, i, place: (0, 0)),
                 pl.BlockSpec(all_weights.shape, lambda h, i, place: (0, 0)),
                 pl.BlockSpec(wedge_columns.shape, lambda h, i, place: (0, 0)),
             ],
             out_specs=[
-                pl.BlockSpec((wide, width), lambda h, i, place: (0, h)),
+                pl.BlockSpec((wide, KB * KB), lambda i, h, place: (0, h * half + i)),
                 pl.BlockSpec((wide, wedge_columns.shape[1]), lambda h, i, place: (0, 0)),
             ],
             scratch_shapes=[pltpu.VMEM((2, wide, rows), BF16)],
@@ -639,7 +639,7 @@
     ).reshape(total_tomos, per_block * LANES)
     flat_refs = references.reshape(wide, -1)
     partial = scores(place, slots, flat_refs, wedge_block, codes)
-    noise = jnp.broadcast_to(inverse_noise[:, None], (part_count, LANES))
+    noise = inverse_noise[:, None]
     posterior, all_weights = weights(
         partial.reshape(-1, part_count, LANES), noise, tomo_axis, cls_axis
     )

time: 110 us -> 110 us (level)
  no operation moved by 1% of the time
where the time goes in v4:
time: 110 us; the launch traced here: 109 us
  Pallas kernels  96.1 us (87%)
  local copies, waits for them, and re-layouts  7.87 us (7%)
  other arithmetic  4.27 us (4%)
    pallas_call x1, Pallas kernels, spectra_slots(): pl.pallas_call(functools.partial(spectra_kernel, tomo_axis, cls_axis), gr...  61 us
    pallas_call x1, Pallas kernels, weights(): pl.pallas_call(functools.partial(weights_kernel, tomo_axis, cls_axis), ou...  16 us
    pallas_call x1, Pallas kernels, sums(): pl.pallas_call(sums_kernel, grid_spec=pltpu.PrefetchScalarGridSpec(num_sc...  11.8 us
    pallas_call x1, Pallas kernels, scores(): pl.pallas_call(score_kernel, grid_spec=pltpu.PrefetchScalarGridSpec(num_s...  7.28 us

profile of v4, /device:TPU:0, one launch (start us, length us, event | category | flops | bytes accessed | tf_op | source)
XLA Modules:
  0.0 109.2 jit_solution(5080282452098469856)
XLA Ops:
  0.6 0.7 pad_add_fusion.place_ref
  1.3 0.7 broadcast_subtract_fusion
  2.0 0.7 broadcast_multiply_fusion
  2.7 0.1 copy.20
  2.8 1.3 %copy.23.noise_ref = f32[8,1]{1,0:T(8,128)} copy(f32[8,1]{0,1:T(1,128)} %bitcast.37) | data formatting | bytes 64 | tf_op jit(solution)/shard_map/broadcast_in_dim | solution.py:642
  4.1 0.7 copy.21
  4.8 0.8 broadcast_add_fusion
  5.6 0.1 add.26
  5.7 0.7 add_add_fusion.code_ref
  6.4 0.8 convert_element_type.18
  7.2 0.1 convert_element_type.13
  7.3 0.7 convert_element_type.15.wedge_ref
  8.0 0.1 dot_general.8
  8.1 0.2 convolution_bitcast_fusion
  8.4 0.8 copy.22.mask_ref
  9.2 61.0 %spectra.1 = (bf16[4,32,16,1024]{3,2,1,0:T(8,128)(2,1)}, s32[32,8,128]{2,1,0:T(8,128)}, bf16[8,32,128]{2,1,0:T(8,128)(2,1)}) custom-call(bf16[512,4096]{1,0:T(8,128)(2,1)} %bitcast.28, bf16[4096,2048]{1,0:T(8,128)(2,1)} %constant.33.clone.th_ref, bf16[4096,2048]{1,0:T(8,128)(2,1)} %constant.34.clone.tl_ref, bf16[512,512]{1,0:T(8,128)(2,1)} %constant.35.clone.wh_ref, ...), custom_call_target="tpu_custom_call" | custom-call | tf_op jit(solution)/shard_map/spectra/pallas_call | solution.py:287
  70.2 0.9 reshape.59
  71.1 0.6 constant_dynamic-slice_fusion.wedge_ref
  71.7 0.1 broadcast_in_dim.22
  71.9 0.9 reshape.60.wedge_ref
  72.8 7.3 %scores.1 = f32[256,128]{1,0:T(8,128)} custom-call(s32[2]{0:T(128)} %pad_add_fusion.place_ref, bf16[4,512,1024]{2,1,0:T(8,128)(2,1)} %bitcast.26, bf16[128,65536]{1,0:T(8,128)(2,1)} %bitcast.25, bf16[32,1024]{1,0:T(8,128)(2,1)} %reshape.60.wedge_ref, s32[256,128]{1,0:T(8,128)} %bitcast.29), custom_call_target="tpu_custom_call" | custom-call | tf_op jit(solution)/shard_map/scores/pallas_call | solution.py:403
  80.1 16.0 %weights.1 = (f32[8,128]{1,0:T(8,128)}, f32[32,8,128]{2,1,0:T(8,128)}) custom-call(f32[32,8,128]{2,1,0:T(8,128)} %bitcast.31, f32[8,1]{1,0:T(8,128)} %copy.23.noise_ref), custom_call_target="tpu_custom_call" | custom-call | tf_op jit(solution)/shard_map/weights/pallas_call | solution.py:510
  96.1 11.8 %sums.1 = (f32[128,8192]{1,0:T(8,128)}, f32[128,128]{1,0:T(8,128)}) custom-call(s32[2]{0:T(128)} %pad_add_fusion.place_ref, bf16[4,512,1024]{2,1,0:T(8,128)(2,1)} %bitcast.27, s32[256,128]{1,0:T(8,128)} %bitcast.30, f32[256,128]{1,0:T(8,128)} %bitcast.34, bf16[32,128]{1,0:T(8,128)(2,1)} %constant_dynamic-slice_fusion.wedge_ref), custom_call_target="tpu_custom_call" | custom-call | tf_op jit(solution)/shard_map/sums/pallas_call | solution.py:561
  107.9 1.3 %copy.28 = f32[8,32]{1,0:T(8,128)} copy(f32[8,32]{1,0:T(8,128)} %bitcast.36) | data formatting | bytes 2048
  (7 shorter events, 0.2 us)
